TPU v7x, 128 devices: a whole 4x4x4 slice. The times are simulated.
128 devices in a mesh: tok: 8 (over x, y_hi), voc: 16 (over y_lo, z, core).
Axes of the slice: x: 4, y: 4 (y_hi: 2, y_lo: 2; y = y_hi * 2 + y_lo), z: 4, core: 2. Of those that a mesh axis runs over, the one named last changes fastest.
Arguments:
- teacher_hidden: bfloat16 [256, 4096], P(None, 'tok'), may hold values from -70 to 70
- teacher_head: bfloat16 [4096, 8, 12288], P('tok', None, 'voc')
- student_hidden: bfloat16 [256, 2, 2560], P(('tok', 'voc')), may hold values from -60 to 60
- student_head: bfloat16 [2560, 98304], P(None, ('tok', 'voc'))
- target_ids: int32 [256, 2], replicated, may hold values from 0 to 98303
Outputs:
- sample_objective: float32 [256, 2], replicated
- grad_hidden: bfloat16 [256, 2, 2560], P(('tok', 'voc'))
- grad_head: bfloat16 [2560, 98304], P(None, ('tok', 'voc'))
All inputs are finite; a program needn't handle non-finite values.
Results may differ from a plain program's by a relative error of at most 0.0044.
Values may be sent and summed in bfloat16 or wider, within the bound.
No kernel may reach another device: no remote copies, remote signals or barrier semaphores. Data moves between devices by JAX's collectives and lax.ppermute only.
A program may use at most 128 MiB of HBM per device.

v0:
```python
import jax
import jax.numpy as jnp
from jax import lax
from jax.experimental import pallas as pl
from jax.experimental.pallas import tpu as pltpu
from jax.sharding import Mesh
from jax.sharding import PartitionSpec as P

TOK = ("xh", "xl", "yh")
VOC = ("yl", "z", "c")
SIZES = (2, 2, 2, 2, 4, 2)
STRIPES = ("yh", "xl", "xh")
WALK = ("z", "yh", "yl", "xh", "xl")
EXCHANGE = ("z", "yh", "xh", "yl", "xl", "c")


def encode(partial):
    stripes, rows, width = partial.shape
    half = width // 2
    peak = jnp.maximum(jnp.max(jnp.abs(partial), axis=2), 1e-30)
    level = jnp.ceil(jnp.log2(peak) * 256.0)
    scale = jnp.exp2(-level / 256.0) * 32766.0
    code = jnp.clip(jnp.round(partial * scale[:, :, None]), -32767.0, 32767.0).astype(jnp.int32)
    words = (code[:, :, :half] << 16) | (code[:, :, half:] & 0xFFFF)
    tail = jnp.zeros((stripes, 8, half), jnp.int32).at[:, 0, :rows].set(level.astype(jnp.int32))
    return jnp.concatenate([words, tail], axis=1)


def row_of(place, core):
    head = (place >> 1) & 1
    row = ((place >> 2) & 3) * 64 + ((place >> 4) & 3) * 16 + (place >> 6) * 4 + core * 2 + (place & 1)
    return row, head


def teacher_kernel(core_ref, words_ref, mine_out, theirs_out, lines_out, sum_ref):
    rows, width = sum_ref.shape
    senders = words_ref.shape[0]
    half = width // 2
    step = 32
    level = jnp.concatenate([words_ref[j, rows : rows + 1, :rows] for j in range(senders)], axis=0)
    scale = jnp.transpose(jnp.exp2(level.astype(jnp.float32) * (1.0 / 256.0)) * (0.5 / 32766.0))
    peaks, totals = [], []
    for at in range(0, rows, step):
        here = pl.ds(at, step)
        low = jnp.zeros((step, half), jnp.float32)
        high = jnp.zeros((step, half), jnp.float32)
        for j in range(senders):
            body = words_ref[j, here, :]
            by = scale[at : at + step, j : j + 1]
            high = high + (body >> 16).astype(jnp.float32) * by
            low = low + ((body << 16) >> 16).astype(jnp.float32) * by
        sum_ref[here, :half] = high
        sum_ref[here, half:] = low
        peak = jnp.maximum(jnp.max(high, axis=1, keepdims=True), jnp.max(low, axis=1, keepdims=True))
        total = jnp.sum(jnp.exp(high - peak), axis=1, keepdims=True)
        total = total + jnp.sum(jnp.exp(low - peak), axis=1, keepdims=True)
        peaks.append(peak)
        totals.append(total)
    peak = jnp.concatenate(peaks, axis=0)
    total = jnp.concatenate(totals, axis=0)
    lane = lax.broadcasted_iota(jnp.int32, (rows, rows), 1)
    place = lax.broadcasted_iota(jnp.int32, (rows, rows), 0)
    eye = lane == place
    first = sum_ref[...].astype(jnp.bfloat16)
    rest = sum_ref[...] - first.astype(jnp.float32)
    second = rest.astype(jnp.bfloat16)
    third = (rest - second.astype(jnp.float32)).astype(jnp.bfloat16)
    for side, out in ((0, mine_out), (1, theirs_out)):
        core = jnp.where(side == 0, core_ref[0], 1 - core_ref[0])
        row, head = row_of(place, core)
        chosen = lane == jnp.minimum(row + head, rows - 1)
        pick = jnp.where(chosen, 1.0, 0.0).astype(jnp.bfloat16)
        moved = jnp.dot(pick, first, preferred_element_type=jnp.float32)
        moved = moved + jnp.dot(pick, second, preferred_element_type=jnp.float32)
        out[...] = moved + jnp.dot(pick, third, preferred_element_type=jnp.float32)
    lines = [jnp.sum(jnp.where(eye, column, 0.0), axis=0, keepdims=True) for column in (peak, total)]
    lines_out[...] = jnp.concatenate(lines + [jnp.zeros((6, rows), jnp.float32)], axis=0)


def cross_kernel(
    core_ref, lines_ref, mine_t_ref, theirs_t_ref, mine_ref, theirs_ref, stats_ref, ids_ref, copies_out, ids_out
):
    rows = mine_ref.shape[0]
    edge = rows // 2
    step = 32
    lane = lax.broadcasted_iota(jnp.int32, (rows, rows), 1)
    place = lax.broadcasted_iota(jnp.int32, (rows, rows), 0)
    ids_out[...] = ids_ref[...]
    crosses = [jnp.zeros((1, rows), jnp.float32), jnp.zeros((1, rows), jnp.float32)]
    for side, teacher, scores in ((0, mine_t_ref, mine_ref), (1, theirs_t_ref, theirs_ref)):
        core = jnp.where(side == 0, core_ref[0], 1 - core_ref[0])
        row, head = row_of(place, core)
        parts = []
        for at in range(0, rows, step):
            here = pl.ds(at, step)
            logits = teacher[here, :]
            weight = jnp.exp(logits - jnp.max(logits, axis=1, keepdims=True))
            parts.append(jnp.sum(weight * (logits - 0.5 * scores[here, :]), axis=1, keepdims=True))
        cross = jnp.concatenate(parts, axis=0)
        for k in (0, 1):
            inside = (lane == row + k) & (head == k)
            crosses[k] = crosses[k] + jnp.sum(jnp.where(inside, cross, 0.0), axis=0, keepdims=True)
    lines = [lines_ref[0:1, :], lines_ref[1:2, :]] + crosses
    tile = jnp.concatenate([line[:, at : at + edge] for line in lines for at in (0, edge)], axis=0)
    rest = jnp.concatenate([stats_ref[...], jnp.zeros((4, edge), jnp.float32)], axis=0)
    copies_out[:, 0:8, :] = jnp.broadcast_to(tile[None], (copies_out.shape[0], 8, edge))
    copies_out[:, 8:16, :] = jnp.broadcast_to(rest[None], (copies_out.shape[0], 8, edge))


def whole(shape):
    return pl.BlockSpec(shape, lambda *_: (0,) * len(shape), pipeline_mode=pl.Buffered(1))


def call(kernel, scalars, operands, results, grant, cost, scratch=()):
    return pl.pallas_call(
        kernel,
        out_shape=tuple(results),
        grid_spec=pltpu.PrefetchScalarGridSpec(
            num_scalar_prefetch=1,
            grid=(1,),
            in_specs=[whole(a.shape) for a in operands],
            out_specs=tuple(whole(a.shape) for a in results),
            scratch_shapes=scratch,
        ),
        compiler_params=pltpu.CompilerParams(vmem_limit_bytes=grant << 20),
        cost_estimate=pl.CostEstimate(flops=cost[0], bytes_accessed=cost[1], transcendentals=cost[2]),
    )(scalars, *operands)


def teacher_sum(scalars, words, rows, width):
    half = jax.ShapeDtypeStruct((rows, width), jnp.float32)
    lines = jax.ShapeDtypeStruct((8, rows), jnp.float32)
    area = rows * width
    scratch = [pltpu.VMEM((rows, width), jnp.float32)]
    return call(teacher_kernel, scalars, (words,), (half, half, lines), 12, (12 * rows * area, 32 * area, area), scratch)


def cross_terms(scalars, operands, devices):
    lines, ids = operands[0], operands[-1]
    copies = jax.ShapeDtypeStruct((devices, 16, lines.shape[1] // 2), jnp.float32)
    area = operands[1].size
    return call(cross_kernel, scalars, operands, (copies, jax.ShapeDtypeStruct(ids.shape, ids.dtype)), 9, (16 * area, 20 * area, 2 * area))


def slope_kernel(core_ref, shares_ref, ids_ref, mine_ref, theirs_ref, mine_t_ref, theirs_t_ref, mine_out, theirs_out, objective_out):
    devices = shares_ref.shape[0]
    rows, width = mine_ref.shape
    edge = rows // 2
    step = 32
    batch = 16
    four = lambda a: jnp.concatenate([a, a, a, a], axis=1)
    top = jnp.max(shares_ref[0:batch, 0:8, :], axis=0)
    for at in range(batch, devices, batch):
        top = jnp.maximum(top, jnp.max(shares_ref[at : at + batch, 0:8, :], axis=0))
    top = jnp.concatenate([top[0:2]] * 4, axis=0)
    sums = jnp.zeros((8, edge), jnp.float32)
    for at in range(0, devices, batch):
        part = shares_ref[at : at + batch, 0:8, :]
        sums = sums + jnp.sum(jnp.exp(four(part[:, 0:2]) - top[None]) * part, axis=0)
    line = lambda a: jnp.concatenate([a[0:1], a[1:2]], axis=1)
    t_total = sums[2:4]
    t_lse = line(top[0:2] + jnp.log(t_total))
    cross = [line(sums[4:6] / t_total), line(sums[6:8] / t_total)]

    ones, taus, targets = [], [], []
    quarter = devices // 4
    kind = lax.broadcasted_iota(jnp.int32, (batch, 8, edge), 1)
    for q in range(4):
        peak = jnp.max(shares_ref[q * quarter : (q + 1) * quarter, 8:16, :], axis=0)[0:1]
        total = jnp.zeros((8, edge), jnp.float32)
        for at in range(q * quarter, (q + 1) * quarter, batch):
            part = shares_ref[at : at + batch, 8:16, :]
            scale = jnp.exp(0.5 * (part[:, 0:1] - peak[None]))
            scale = jnp.broadcast_to(scale, part.shape)
            scale = jnp.where(kind == 1, scale * scale, jnp.where(kind == 2, scale, 1.0))
            total = total + jnp.sum(scale * part, axis=0)
        ones.append(peak + jnp.log(total[1:2]))
        taus.append(0.5 * peak + jnp.log(total[2:3]))
        targets.append(total[3:4])
    norms = jnp.transpose(jnp.concatenate(ones + taus + targets + targets, axis=0))

    lane = lax.broadcasted_iota(jnp.int32, (rows, rows), 1)
    place = lax.broadcasted_iota(jnp.int32, (rows, rows), 0)
    objective = [jnp.zeros((1, rows), jnp.float32), jnp.zeros((1, rows), jnp.float32)]
    base = core_ref[1]
    columns = lax.broadcasted_iota(jnp.int32, (step, width), 1) + base
    for side, scores, teacher, out in ((0, mine_ref, mine_t_ref, mine_out), (1, theirs_ref, theirs_t_ref, theirs_out)):
        first = (core_ref[0] == 0) == (side == 0)
        core = jnp.where(first, 0, 1)

        def column(n):
            low = jnp.concatenate([norms[:, n : n + 1], norms[:, n + 1 : n + 2]], axis=0)
            high = jnp.concatenate([norms[:, n + 2 : n + 3], norms[:, n + 3 : n + 4]], axis=0)
            return jnp.where(first, low, high)

        one, tau, target = column(0), column(4), column(8)
        row, head = row_of(place, core)
        chosen = lane == jnp.minimum(row + head, rows - 1)
        lse = jnp.sum(jnp.where(chosen, t_lse, 0.0), axis=1, keepdims=True)
        mixed = jnp.where(head == 0, cross[0], cross[1])
        mixed = jnp.sum(jnp.where(chosen, mixed, 0.0), axis=1, keepdims=True)
        weight = jnp.where((head[:, 0:1] == 1) & (row[:, 0:1] == rows - 1), 0.0, 1.0)
        loss = weight * (2.0 * (mixed - lse + tau) + 0.5 * (one - target))
        for k in (0, 1):
            inside = (lane == row) & (head == k)
            objective[k] = objective[k] + jnp.sum(jnp.where(inside, loss, 0.0), axis=0, keepdims=True)
        ids = jnp.where(first, ids_ref[0], ids_ref[1])
        for at in range(0, rows, step):
            here = pl.ds(at, step)
            part = slice(at, at + step)
            score = scores[here, :]
            grad = jnp.exp(0.5 * score - tau[part]) - jnp.exp(teacher[here, :] - lse[part])
            hit = jnp.where(columns == ids[part], 1.0, 0.0)
            grad = weight[part] * (grad + 0.5 * (jnp.exp(score - one[part]) - hit))
            out[here, :] = grad.astype(jnp.bfloat16)
    objective_out[...] = jnp.concatenate(objective + [jnp.zeros((6, rows), jnp.float32)], axis=0)


def slopes(scalars, *operands):
    half = jax.ShapeDtypeStruct(operands[2].shape, jnp.bfloat16)
    lines = jax.ShapeDtypeStruct((8, half.shape[0]), jnp.float32)
    area = operands[2].size
    return call(slope_kernel, scalars, operands, (half, half, lines), 9, (40 * area, 24 * area, 6 * area))


def merge(parts):
    peak = jnp.max(parts[:, 0], axis=0)
    scale = jnp.exp((parts[:, 0] - peak) * 0.5)
    return jnp.stack(
        [
            peak,
            jnp.sum(parts[:, 1] * (scale * scale), axis=0),
            jnp.sum(parts[:, 2] * scale, axis=0),
            jnp.sum(parts[:, 3], axis=0),
        ]
    )


def ring_gather(block, axes):
    size = lax.axis_size(axes)
    here = lax.axis_index(axes)
    whole = jnp.zeros((size,) + block.shape, block.dtype)
    whole = lax.dynamic_update_index_in_dim(whole, block, here, 0)
    for step in range(1, size):
        taken = lax.ppermute(block, axes, [(i, (i + step) % size) for i in range(size)])
        whole = lax.dynamic_update_index_in_dim(whole, taken, (here + size - step) % size, 0)
    return whole.reshape((size * block.shape[0],) + block.shape[1:])


def everywhere(value, axes, count):
    copies = jnp.broadcast_to(value, (count,) + value.shape)
    return lax.all_to_all(copies, axes, 0, 0, tiled=True)


def local(teacher_hidden, teacher_head, student_hidden, student_head, target_ids):
    core = lax.axis_index("c")
    chips = lax.axis_size(WALK)
    devices = lax.axis_size(EXCHANGE)
    stripes = teacher_head.shape[1]
    voc = teacher_head.shape[2]
    rows = teacher_hidden.shape[0]
    width = student_head.shape[0]
    base = lax.axis_index(TOK + VOC) * voc
    pair = [(0, 1), (1, 0)]

    partial = jnp.einsum("rd,dsv->srv", teacher_hidden, teacher_head, preferred_element_type=jnp.float32)
    words = encode(partial)
    words = words.reshape((2, 2, 2) + words.shape[1:]).transpose(2, 1, 0, 3, 4).reshape(words.shape)
    words = lax.all_to_all(words, STRIPES, 0, 0, tiled=True)

    plane = jnp.swapaxes(student_hidden, 0, 1).reshape(4, width)
    plane = everywhere(plane, ("yh", "yl", "xh", "xl"), 16).reshape(64, width)

    own = ring_gather(plane, "z")
    other = lax.ppermute(own, "c", pair)

    order = target_ids.reshape(4, 4, 4, 2, 2, 2)
    order = jnp.transpose(order, (3, 2, 1, 0, 5, 4)).reshape(2, rows, 1)
    columns = lax.broadcasted_iota(jnp.int32, (1, voc), 1) + base

    def student(hidden, side):
        scores = jnp.dot(hidden, student_head, preferred_element_type=jnp.float32)
        match = columns == jnp.where(side == 0, order[0], order[1])
        top = jnp.max(scores, axis=1, keepdims=True)
        powers = jnp.exp((scores - top) * 0.5)
        stats = jnp.stack(
            [
                top[:, 0],
                jnp.sum(powers * powers, axis=1),
                jnp.sum(powers, axis=1),
                jnp.sum(jnp.where(match, scores, 0.0), axis=1),
            ]
        )
        return scores, stats

    own_scores, own_stats = student(own, core)
    other_scores, other_stats = student(other, 1 - core)
    stats = jnp.stack(
        [jnp.where(core == 0, own_stats, other_stats), jnp.where(core == 0, other_stats, own_stats)], axis=1
    ).reshape(4, 2 * rows)
    stats = stats + 0.0 * words[0, 0, 0].astype(jnp.float32)
    around = [stats] + [lax.ppermute(stats, "z", [(i, (i + j) % 4) for i in range(4)]) for j in (1, 2, 3)]
    stats = merge(jnp.stack(around)).reshape(4, 4, rows // 2)
    stats = lax.dynamic_index_in_dim(stats, lax.axis_index("z"), 1, False)

    scalars = jnp.stack([core, base])
    own_teacher, other_teacher, lines = teacher_sum(scalars, words, rows, voc)
    copies, order = cross_terms(
        scalars, (lines, own_teacher, other_teacher, own_scores, other_scores, stats, order), devices
    )
    hidden = jnp.concatenate([own, other], axis=0)
    copies, hidden, order = lax.optimization_barrier((copies, hidden, order))
    shares = lax.all_to_all(copies, EXCHANGE, 0, 0, tiled=True)
    own_grad, other_grad, objective = slopes(
        scalars, shares, order, own_scores, other_scores, own_teacher, other_teacher
    )

    contract = (((1,), (1,)), ((), ()))
    give = lax.dot_general(other_grad, student_head, contract, preferred_element_type=jnp.float32)
    taken = lax.ppermute(give, "c", pair)
    keep = lax.dot_general(own_grad, student_head, contract, preferred_element_type=jnp.float32)
    grad = jnp.concatenate([own_grad, other_grad], axis=0)
    grad_head = lax.dot_general(
        hidden, grad, (((0,), (0,)), ((), ())), preferred_element_type=jnp.float32
    ).astype(jnp.bfloat16)
    objective = objective[:2].T

    share = (keep + taken).astype(jnp.bfloat16).reshape(chips, 4, width)
    share, grad_head, objective = lax.optimization_barrier((share, grad_head, objective))
    share = lax.all_to_all(share, WALK, 0, 0, tiled=True)
    grad_hidden = jnp.sum(share.astype(jnp.float32), axis=0).astype(jnp.bfloat16)
    grad_hidden = jnp.swapaxes(grad_hidden.reshape(2, 2, width), 0, 1)
    return objective, grad_hidden, grad_head


def solution(mesh):
    fine = Mesh(mesh.devices.reshape(SIZES), TOK + VOC)
    return jax.shard_map(
        local,
        mesh=fine,
        in_specs=(
            P(None, TOK),
            P(TOK, None, VOC),
            P(TOK + VOC, None, None),
            P(None, TOK + VOC),
            P(),
        ),
        out_specs=(P(), P(TOK + VOC, None, None), P(None, TOK + VOC)),
        check_vma=False,
    )
```

profile of v0, /device:TPU:0, one launch (start us, length us, event | category | flops | bytes accessed | tf_op | source)
XLA Modules:
  0.0 157.6 jit_solution(9275716797161202956)
XLA Ops:
  2.3 7.2 %all-to-all-start.1 = ((bf16[16,4,2560]{2,1,0:T(4,128)(2,1)}), bf16[16,4,2560]{2,1,0:T(4,128)(2,1)}, u32[]{:S(2)}, u32[]{:S(2)}) async-start(bf16[16,4,2560]{2,1,0:T(4,128)(2,1)} %broadcast_in_dim.30), calls=%async_computation.1 | async-start | bytes 655360 | tf_op jit(solution)/shard_map/all_to_all | solution.py:252
  9.4 5.7 %abs_reduce_fusion = (f32[8,256]{1,0:T(8,128)S(1)}, f32[8,768,256]{1,2,0:T(8,128)S(1)}) fusion(bf16[512,8,768]{2,1,0:T(8,128)(2,1)} %param.8, bf16[256,512]{1,0:T(8,128)(2,1)S(1)} %copy-done), kind=kOutput, calls=%fused_computation.3 | convolution fusion | flops 1613756416 | bytes 12853248 | tf_op jit(solution)/shard_map/rd,dsv->srv/dot_general | solution.py:266
  16.6 1.9 %copy.24 = s32[2,2,2,264,384]{4,3,0,1,2:T(8,128)} copy(s32[2,2,2,264,384]{4,3,2,1,0:T(8,128)S(1)} %bitcast.79) | data formatting | bytes 6488064 | tf_op jit(solution)/shard_map/reshape | solution.py:268
  18.9 6.7 %all-to-all-start = ((s32[8,264,384]{2,1,0:T(8,128)}), s32[8,264,384]{2,1,0:T(8,128)S(1)}, u32[]{:S(2)}, u32[]{:S(2)}) async-start(s32[8,264,384]{2,1,0:T(8,128)} %bitcast.78), calls=%async_computation | async-start | bytes 6488064 | tf_op jit(solution)/shard_map/all_to_all | solution.py:269
  25.5 1.8 %reshape.399 = bf16[64,2560]{1,0:T(8,128)(2,1)} reshape(bf16[16,4,2560]{2,1,0:T(4,128)(2,1)} %all-to-all-done.1) | data formatting | bytes 655360 | tf_op jit(solution)/shard_map/reshape | solution.py:272
  27.3 1.9 %collective-permute-start = (bf16[64,2560]{1,0:T(8,128)(2,1)}, bf16[64,2560]{1,0:T(8,128)(2,1)}, u32[]{:S(2)}, u32[]{:S(2)}) collective-permute-start(bf16[64,2560]{1,0:T(8,128)(2,1)} %reshape.399), channel_id=1, source_target_pairs={{0,2},{2,4},{4,6},{6,0},{1,3},{3,5},{5,7},{7,1},{8,10},{10,12},{12... | collective-permute-start | bytes 983048 | tf_op jit(solution)/shard_map/ppermute | solution.py:245
  29.2 3.6 %collective-permute-start.1 = (bf16[64,2560]{1,0:T(8,128)(2,1)}, bf16[64,2560]{1,0:T(8,128)(2,1)}, u32[]{:S(2)}, u32[]{:S(2)}) collective-permute-start(bf16[64,2560]{1,0:T(8,128)(2,1)} %reshape.399), channel_id=1, source_target_pairs={{0,4},{2,6},{4,0},{6,2},{1,5},{3,7},{5,1},{7,3},{8,12},{10,14},{12... | collective-permute-start | bytes 983048 | tf_op jit(solution)/shard_map/ppermute | solution.py:245
  33.8 1.8 %broadcast_in_dim.31 = bf16[1,64,2560]{2,1,0:T(8,128)(2,1)} reshape(bf16[16,4,2560]{2,1,0:T(4,128)(2,1)} %all-to-all-done.1) | data formatting | bytes 655360 | tf_op jit(solution)/shard_map/jit(dynamic_update_index_in_dim)/broadcast_in_dim | solution.py:243
  35.6 1.2 broadcast_in_dim.29
  36.8 1.7 %constant_dynamic-update-slice_fusion = bf16[4,64,2560]{2,1,0:T(8,128)(2,1)} fusion(bf16[4,64,2560]{2,1,0:T(8,128)(2,1)} %broadcast_in_dim.29, bf16[1,64,2560]{2,1,0:T(8,128)(2,1)} %broadcast_in_dim.31, s32[]{:T(128)S(6)} %select_n.93), kind=kLoop, calls=%fused_computation.59 | loop fusion | bytes 655364 | tf_op jit(solution)/shard_map/jit(dynamic_update_index_in_dim)/dynamic_update_slice | solution.py:243
  39.4 1.7 %bitcast_dynamic-update-slice_fusion.2 = bf16[4,64,2560]{2,1,0:T(8,128)(2,1)} fusion(bf16[4,64,2560]{2,1,0:T(8,128)(2,1)} %constant_dynamic-update-slice_fusion, s32[]{:T(128)S(6)} %select_n.95, bf16[64,2560]{1,0:T(8,128)(2,1)} %collective-permute-done), kind=kLoop, calls=%fused_computation.25 | loop fusion | bytes 655364 | tf_op jit(solution)/shard_map/jit(dynamic_update_index_in_dim)/dynamic_update_slice | solution.py:246
  41.1 5.6 %collective-permute-done.1 = bf16[64,2560]{1,0:T(8,128)(2,1)} collective-permute-done((bf16[64,2560]{1,0:T(8,128)(2,1)}, bf16[64,2560]{1,0:T(8,128)(2,1)}, u32[]{:S(2)}, u32[]{:S(2)}) %collective-permute-start.1) | collective-permute-done | bytes 327712 | tf_op jit(solution)/shard_map/ppermute | solution.py:245
  46.7 1.7 %bitcast_dynamic-update-slice_fusion.1 = bf16[4,64,2560]{2,1,0:T(8,128)(2,1)} fusion(bf16[4,64,2560]{2,1,0:T(8,128)(2,1)} %bitcast_dynamic-update-slice_fusion.2, s32[]{:T(128)S(6)} %select_n.97, bf16[64,2560]{1,0:T(8,128)(2,1)} %collective-permute-done.1), kind=kLoop, calls=%fused_computation.24 | loop fusion | bytes 655364 | tf_op jit(solution)/shard_map/jit(dynamic_update_index_in_dim)/dynamic_update_slice | solution.py:246
  48.5 1.7 %bitcast_dynamic-update-slice_fusion = bf16[4,64,2560]{2,1,0:T(8,128)(2,1)} fusion(bf16[4,64,2560]{2,1,0:T(8,128)(2,1)} %bitcast_dynamic-update-slice_fusion.1, s32[]{:T(128)S(6)} %select_n.99, bf16[64,2560]{1,0:T(8,128)(2,1)} %collective-permute-done.2), kind=kLoop, calls=%fused_computation.23 | loop fusion | bytes 655364 | tf_op jit(solution)/shard_map/jit(dynamic_update_index_in_dim)/dynamic_update_slice | solution.py:246
  51.0 1.6 %copy.30 = s32[2,4,4,4,2,2]{5,4,3,2,1,0:T(2,128)} copy(s32[2,4,4,4,2,2]{5,0,1,2,3,4:T(2,128)} %bitcast.80) | data formatting | bytes 4096 | tf_op jit(solution)/shard_map/transpose | solution.py:278
  52.7 1.7 %broadcast_select_fusion = (s32[1,4,4,4,2,2]{5,0,1,2,3,4:T(1,128)S(1)}, s32[1,4,4,4,2,2]{5,0,1,2,3,4:T(1,128)}) fusion(pred[]{:T(512)S(6)} %eq.40, s32[2,4,4,4,2,2]{5,0,1,2,3,4:T(2,128)} %bitcast.81, pred[]{:T(512)S(6)} %eq.18), kind=kLoop, calls=%fused_computation.27 | loop fusion | flops 512 | bytes 4098 | tf_op jit(solution)/shard_map/jit(_where)/select_n | solution.py:283
  56.1 1.5 copy.26
  58.6 1.8 %reshape.407.ids_ref = s32[2,256,1]{2,1,0:T(8,128)} reshape(s32[2,4,4,4,2,2]{5,4,3,2,1,0:T(2,128)} %copy.30) | data formatting | bytes 4096 | tf_op jit(solution)/shard_map/reshape | solution.py:278
  60.5 3.9 %fusion.23 = (f32[256]{0:T(256)S(1)}, f32[256,768]{1,0:T(8,128)S(1)}) fusion(bf16[256,2560]{1,0:T(8,128)(2,1)} %bitcast.11, bf16[2560,768]{1,0:T(8,128)(2,1)} %param.10), kind=kOutput, calls=%fused_computation.63 | convolution fusion | flops 1006829312 | bytes 6030336 | tf_op jit(solution)/shard_map/dot_general | solution.py:282
  64.4 2.9 %fusion.22 = (f32[256]{0:T(256)S(1)}, f32[256,768]{1,0:T(8,128)S(1)}) fusion(bf16[256,2560]{1,0:T(8,128)(2,1)} %collective-permute-done.3, bf16[2560,768]{1,0:T(8,128)(2,1)S(1)} %copy-done.12), kind=kOutput, calls=%fused_computation.62 | convolution fusion | flops 1006829312 | bytes 6030336 | tf_op jit(solution)/shard_map/dot_general | solution.py:282
  68.2 3.4 %pad_maximum_fusion = bf16[512,2560]{1,0:T(8,128)(2,1)} fusion(bf16[256,2560]{1,0:T(8,128)(2,1)} %collective-permute-done.3, bf16[256,2560]{1,0:T(8,128)(2,1)} %bitcast.11), kind=kLoop, calls=%fused_computation.11 | loop fusion | flops 5242880 | bytes 5242880 | tf_op jit(solution)/shard_map/concatenate | solution.py:311
  73.2 1.9 %collective-permute-start.5 = (f32[4,512]{1,0:T(4,128)S(1)}, f32[4,512]{1,0:T(4,128)}, u32[]{:S(2)}, u32[]{:S(2)}) collective-permute-start(f32[4,512]{1,0:T(4,128)S(1)} %bitcast.86), channel_id=1, source_target_pairs={{0,4},{2,6},{4,0},{6,2},{1,5},{3,7},{5,1},{7,3},{8,12},{10,14},{12... | collective-permute-start | bytes 24584 | tf_op jit(solution)/shard_map/ppermute | solution.py:302
  75.1 1.3 collective-permute-start.4
  76.4 2.6 %shard_map.76 = (f32[256,768]{1,0:T(8,128)S(1)}, f32[256,768]{1,0:T(8,128)S(1)}, f32[8,256]{1,0:T(8,128)S(1)}) custom-call(s32[2]{0:T(128)S(1)} %pad_add_fusion.1.core_ref, s32[8,264,384]{2,1,0:T(8,128)S(1)} %all-to-all-done.words_ref), custom_call_target="tpu_custom_call" | custom-call | flops 603979776 | bytes 6291456 | tf_op jit(solution)/shard_map/pallas_call | solution.py:115
  87.2 1.4 shard_map.77
  88.6 28.6 %all_to_all.20.shares_ref = f32[128,16,128]{2,1,0:T(8,128)S(1)} all-to-all(f32[128,16,128]{2,1,0:T(8,128)S(1)} %get-tuple-element.34), channel_id=1, replica_groups=mesh['xh'=2,'xl'=2,'yh'=2,'yl'=2,'z'=4,'c'=2] {'z','yh','xh','yl','xl','c'}, dimensions={0} | all-to-all | bytes 2097152 | tf_op jit(solution)/shard_map/all_to_all | solution.py:313
  117.2 1.1 copy-done.3
  119.5 2.6 %shard_map.78 = (bf16[256,768]{1,0:T(8,128)(2,1)S(1)}, bf16[256,768]{1,0:T(8,128)(2,1)S(1)}, f32[8,256]{1,0:T(8,128)S(1)}) custom-call(s32[2]{0:T(128)S(1)} %pad_add_fusion.1.core_ref, f32[128,16,128]{2,1,0:T(8,128)S(1)} %all_to_all.20.shares_ref, s32[2,256,1]{2,1,0:T(8,128)S(1)} %get-tuple-element.35.ids_ref, f32[256,768]{1,0:T(8,128)S(1)} %copy-done.3, ...), custom_call_target="tpu_custom_call" | custom-call | flops 7864320 | bytes 4718592 | tf_op jit(solution)/shard_map/pallas_call | solution.py:115
  122.1 1.2 fusion.24
  124.0 4.2 %convolution_convert_fusion = bf16[2560,768]{1,0:T(8,128)(2,1)} fusion(bf16[512,2560]{1,0:T(8,128)(2,1)S(1)} %copy-done.14, bf16[256,768]{1,0:T(8,128)(2,1)S(1)} %get-tuple-element.37, bf16[256,768]{1,0:T(8,128)(2,1)S(1)} %get-tuple-element.36), kind=kOutput, calls=%fused_computation.4 | convolution fusion | flops 2016804864 | bytes 7340032 | tf_op jit(solution)/shard_map/dot_general | solution.py:323
  128.3 1.2 fusion.2
  129.9 26.5 %all_to_all.21 = bf16[64,4,2560]{2,1,0:T(4,128)(2,1)S(1)} all-to-all(bf16[64,4,2560]{2,1,0:T(4,128)(2,1)S(1)} %reshape.403), channel_id=1, replica_groups=mesh['xh'=2,'xl'=2,'yh'=2,'yl'=2,'z'=4,'c'=2] {'z','yh','yl','xh','xl'}, dimensions={0} | all-to-all | bytes 2621440 | tf_op jit(solution)/shard_map/all_to_all | solution.py:330
  (78 shorter events, 22.3 us)
Async XLA Ops:
  0.6 8.8 %copy-start = (bf16[256,512]{1,0:T(8,128)(2,1)S(1)}, bf16[256,512]{1,0:T(8,128)(2,1)}, u32[]{:S(2)}) copy-start(bf16[256,512]{1,0:T(8,128)(2,1)} %param.7) | copy-start | bytes 786436
  2.3 16.6 %all-to-all-start.1 = ((bf16[16,4,2560]{2,1,0:T(4,128)(2,1)}), bf16[16,4,2560]{2,1,0:T(4,128)(2,1)}, u32[]{:S(2)}, u32[]{:S(2)}) async-start(bf16[16,4,2560]{2,1,0:T(4,128)(2,1)} %broadcast_in_dim.30), calls=%async_computation.1 | async-start | bytes 655360 | tf_op jit(solution)/shard_map/all_to_all | solution.py:252
  18.9 52.7 %all-to-all-start = ((s32[8,264,384]{2,1,0:T(8,128)}), s32[8,264,384]{2,1,0:T(8,128)S(1)}, u32[]{:S(2)}, u32[]{:S(2)}) async-start(s32[8,264,384]{2,1,0:T(8,128)} %bitcast.78), calls=%async_computation | async-start | bytes 6488064 | tf_op jit(solution)/shard_map/all_to_all | solution.py:269
  25.5 24.6 %copy-start.15 = (s32[256,2]{0,1:T(2,128)S(1)}, s32[256,2]{0,1:T(2,128)}, u32[]{:S(2)}) copy-start(s32[256,2]{0,1:T(2,128)} %param.11) | copy-start | bytes 6148
  27.3 12.1 %collective-permute-start = (bf16[64,2560]{1,0:T(8,128)(2,1)}, bf16[64,2560]{1,0:T(8,128)(2,1)}, u32[]{:S(2)}, u32[]{:S(2)}) collective-permute-start(bf16[64,2560]{1,0:T(8,128)(2,1)} %reshape.399), channel_id=1, source_target_pairs={{0,2},{2,4},{4,6},{6,0},{1,3},{3,5},{5,7},{7,1},{8,10},{10,12},{12... | collective-permute-start | bytes 983048 | tf_op jit(solution)/shard_map/ppermute | solution.py:245
  29.2 17.5 %collective-permute-start.1 = (bf16[64,2560]{1,0:T(8,128)(2,1)}, bf16[64,2560]{1,0:T(8,128)(2,1)}, u32[]{:S(2)}, u32[]{:S(2)}) collective-permute-start(bf16[64,2560]{1,0:T(8,128)(2,1)} %reshape.399), channel_id=1, source_target_pairs={{0,4},{2,6},{4,0},{6,2},{1,5},{3,7},{5,1},{7,3},{8,12},{10,14},{12... | collective-permute-start | bytes 983048 | tf_op jit(solution)/shard_map/ppermute | solution.py:245
  32.8 15.6 %collective-permute-start.2 = (bf16[64,2560]{1,0:T(8,128)(2,1)}, bf16[64,2560]{1,0:T(8,128)(2,1)}, u32[]{:S(2)}, u32[]{:S(2)}) collective-permute-start(bf16[64,2560]{1,0:T(8,128)(2,1)} %reshape.399), channel_id=1, source_target_pairs={{0,6},{2,0},{4,2},{6,4},{1,7},{3,1},{5,3},{7,5},{8,14},{10,8},{12,... | collective-permute-start | bytes 983048 | tf_op jit(solution)/shard_map/ppermute | solution.py:245
  50.2 14.2 %collective-permute-start.3 = (bf16[256,2560]{1,0:T(8,128)(2,1)}, bf16[256,2560]{1,0:T(8,128)(2,1)}, u32[]{:S(2)}, u32[]{:S(2)}) collective-permute-start(bf16[256,2560]{1,0:T(8,128)(2,1)} %bitcast.11), channel_id=1, source_target_pairs={{0,1},{1,0},{2,3},{3,2},{4,5},{5,4},{6,7},{7,6},{8,9},{9,8},{10,11... | collective-permute-start | bytes 3932168 | tf_op jit(solution)/shard_map/ppermute | solution.py:275
  60.5 3.9 %copy-start.12 = (bf16[2560,768]{1,0:T(8,128)(2,1)S(1)}, bf16[2560,768]{1,0:T(8,128)(2,1)}, u32[]{:S(2)}) copy-start(bf16[2560,768]{1,0:T(8,128)(2,1)} %param.10) | copy-start | bytes 11796484
  64.4 2.9 %copy-start.1 = (f32[256,768]{1,0:T(8,128)}, f32[256,768]{1,0:T(8,128)S(1)}, u32[]{:S(2)}) copy-start(f32[256,768]{1,0:T(8,128)S(1)} %get-tuple-element.74.mine_ref) | copy-start | bytes 2359300
  67.3 0.9 copy-start.4
  72.8 8.8 %collective-permute-start.6 = (f32[4,512]{1,0:T(4,128)S(1)}, f32[4,512]{1,0:T(4,128)S(1)}, u32[]{:S(2)}, u32[]{:S(2)}) collective-permute-start(f32[4,512]{1,0:T(4,128)S(1)} %bitcast.85), channel_id=1, source_target_pairs={{0,6},{2,0},{4,2},{6,4},{1,7},{3,1},{5,3},{7,5},{8,14},{10,8},{12,... | collective-permute-start | bytes 24584 | tf_op jit(solution)/shard_map/ppermute | solution.py:302
  73.2 7.6 %collective-permute-start.5 = (f32[4,512]{1,0:T(4,128)S(1)}, f32[4,512]{1,0:T(4,128)}, u32[]{:S(2)}, u32[]{:S(2)}) collective-permute-start(f32[4,512]{1,0:T(4,128)S(1)} %bitcast.86), channel_id=1, source_target_pairs={{0,4},{2,6},{4,0},{6,2},{1,5},{3,7},{5,1},{7,3},{8,12},{10,14},{12... | collective-permute-start | bytes 24584 | tf_op jit(solution)/shard_map/ppermute | solution.py:302
  75.1 6.4 %collective-permute-start.4 = (f32[4,512]{1,0:T(4,128)S(1)}, f32[4,512]{1,0:T(4,128)S(1)}, u32[]{:S(2)}, u32[]{:S(2)}) collective-permute-start(f32[4,512]{1,0:T(4,128)S(1)} %bitcast.87), channel_id=1, source_target_pairs={{0,2},{2,4},{4,6},{6,0},{1,3},{3,5},{5,7},{7,1},{8,10},{10,12},{12... | collective-permute-start | bytes 24584 | tf_op jit(solution)/shard_map/ppermute | solution.py:302
  79.0 0.9 copy-start.7
  79.9 0.9 copy-start.9
  81.7 1.1 copy-start.2
  82.8 1.1 copy-start.5
  84.0 1.1 copy-start.8
  85.1 1.1 copy-start.10
  86.2 0.9 copy-start.11
  117.2 1.1 copy-start.3
  118.4 1.1 copy-start.6
  119.5 2.6 %copy-start.13 = (bf16[2560,768]{1,0:T(8,128)(2,1)S(1)}, bf16[2560,768]{1,0:T(8,128)(2,1)}, u32[]{:S(2)}) copy-start(bf16[2560,768]{1,0:T(8,128)(2,1)} %param.10) | copy-start | bytes 11796484
  122.1 1.9 %copy-start.14 = (bf16[512,2560]{1,0:T(8,128)(2,1)S(1)}, bf16[512,2560]{1,0:T(8,128)(2,1)}, u32[]{:S(2)}) copy-start(bf16[512,2560]{1,0:T(8,128)(2,1)} %pad_maximum_fusion) | copy-start | bytes 7864324
  123.3 5.0 %collective-permute-start.7 = (f32[256,2560]{1,0:T(8,128)S(1)}, f32[256,2560]{1,0:T(8,128)S(1)}, u32[]{:S(2)}, u32[]{:S(2)}) collective-permute-start(f32[256,2560]{1,0:T(8,128)S(1)} %fusion.24), channel_id=1, source_target_pairs={{0,1},{1,0},{2,3},{3,2},{4,5},{5,4},{6,7},{7,6},{8,9},{9,8},{10,11... | collective-permute-start | bytes 7864328 | tf_op jit(solution)/shard_map/ppermute | solution.py:320
where the time goes:
time: 159 us; the launch traced here: 158 us
  blocking collectives  55.1 us (35%)
  local copies, waits for them, and re-layouts  36.1 us (23%)
  starting transfers between devices  24.1 us (15%)
  matrix products  19.1 us (12%)
  other arithmetic  7.99 us (5%)
  waiting for transfers between devices  7.06 us (4%)
  Pallas kernels  6.57 us (4%)
  between operations  1.65 us (1%)
    all_to_all x1, blocking collectives, local(): shares = lax.all_to_all(copies, EXCHANGE, 0, 0, tiled=True)  28.6 us
    all_to_all x1, blocking collectives, local(): share = lax.all_to_all(share, WALK, 0, 0, tiled=True)  26.5 us
    unnamed x34, local copies, waits for them, and re-layouts  10.3 us
    all_to_all x1, starting transfers between devices, everywhere(): return lax.all_to_all(copies, axes, 0, 0, tiled=True)  7.16 us
    dot_general x2, matrix products, student(): scores = jnp.dot(hidden, student_head, preferred_element_type=jnp.float32)  6.77 us
    all_to_all x1, starting transfers between devices, local(): words = lax.all_to_all(words, STRIPES, 0, 0, tiled=True)  6.67 us
    pallas_call x3, Pallas kernels, call(): pl.pallas_call(kernel, out_shape=tuple(results), grid_spec=pltpu.Prefetch...  6.57 us
    ppermute x3, starting transfers between devices, ring_gather(): lax.ppermute(block, axes, [(i, (i + step) % size) for i in range(size)])  6.51 us
  transfers between devices with their start and end apart: 10, of which 4 were waited for; matrix products, arithmetic and copies ran while one was open for 30% of the time, Pallas kernels for 2%

commit v1 on v0

--- a/solution.py
+++ b/solution.py
@@ -1,3 +1,5 @@
+import functools
+
 import jax
 import jax.numpy as jnp
 from jax import lax
@@ -9,9 +11,10 @@
 TOK = ("xh", "xl", "yh")
 VOC = ("yl", "z", "c")
 SIZES = (2, 2, 2, 2, 4, 2)
+GRANT = 14
 STRIPES = ("yh", "xl", "xh")
 WALK = ("z", "yh", "yl", "xh", "xl")
-EXCHANGE = ("z", "yh", "xh", "yl", "xl", "c")
+EXCHANGE = ("z", "yh", "xh", "yl", "xl")
 
 
 def encode(partial):
@@ -32,7 +35,7 @@
     return row, head
 
 
-def teacher_kernel(core_ref, words_ref, mine_out, theirs_out, lines_out, sum_ref):
+def teacher_kernel(core_ref, words_ref, mine_ref, theirs_ref, mine_out, theirs_out, tile_out, sum_ref):
     rows, width = sum_ref.shape
     senders = words_ref.shape[0]
     half = width // 2
@@ -65,7 +68,8 @@
     rest = sum_ref[...] - first.astype(jnp.float32)
     second = rest.astype(jnp.bfloat16)
     third = (rest - second.astype(jnp.float32)).astype(jnp.bfloat16)
-    for side, out in ((0, mine_out), (1, theirs_out)):
+    crosses = [jnp.zeros((1, rows), jnp.float32), jnp.zeros((1, rows), jnp.float32)]
+    for side, scores, out in ((0, mine_ref, mine_out), (1, theirs_ref, theirs_out)):
         core = jnp.where(side == 0, core_ref[0], 1 - core_ref[0])
         row, head = row_of(place, core)
         chosen = lane == jnp.minimum(row + head, rows - 1)
@@ -73,38 +77,64 @@
         moved = jnp.dot(pick, first, preferred_element_type=jnp.float32)
         moved = moved + jnp.dot(pick, second, preferred_element_type=jnp.float32)
         out[...] = moved + jnp.dot(pick, third, preferred_element_type=jnp.float32)
-    lines = [jnp.sum(jnp.where(eye, column, 0.0), axis=0, keepdims=True) for column in (peak, total)]
-    lines_out[...] = jnp.concatenate(lines + [jnp.zeros((6, rows), jnp.float32)], axis=0)
-
-
-def cross_kernel(
-    core_ref, lines_ref, mine_t_ref, theirs_t_ref, mine_ref, theirs_ref, stats_ref, ids_ref, copies_out, ids_out
-):
-    rows = mine_ref.shape[0]
-    edge = rows // 2
-    step = 32
-    lane = lax.broadcasted_iota(jnp.int32, (rows, rows), 1)
-    place = lax.broadcasted_iota(jnp.int32, (rows, rows), 0)
-    ids_out[...] = ids_ref[...]
-    crosses = [jnp.zeros((1, rows), jnp.float32), jnp.zeros((1, rows), jnp.float32)]
-    for side, teacher, scores in ((0, mine_t_ref, mine_ref), (1, theirs_t_ref, theirs_ref)):
-        core = jnp.where(side == 0, core_ref[0], 1 - core_ref[0])
-        row, head = row_of(place, core)
         parts = []
         for at in range(0, rows, step):
             here = pl.ds(at, step)
-            logits = teacher[here, :]
+            logits = out[here, :]
             weight = jnp.exp(logits - jnp.max(logits, axis=1, keepdims=True))
             parts.append(jnp.sum(weight * (logits - 0.5 * scores[here, :]), axis=1, keepdims=True))
         cross = jnp.concatenate(parts, axis=0)
         for k in (0, 1):
             inside = (lane == row + k) & (head == k)
             crosses[k] = crosses[k] + jnp.sum(jnp.where(inside, cross, 0.0), axis=0, keepdims=True)
-    lines = [lines_ref[0:1, :], lines_ref[1:2, :]] + crosses
-    tile = jnp.concatenate([line[:, at : at + edge] for line in lines for at in (0, edge)], axis=0)
-    rest = jnp.concatenate([stats_ref[...], jnp.zeros((4, edge), jnp.float32)], axis=0)
-    copies_out[:, 0:8, :] = jnp.broadcast_to(tile[None], (copies_out.shape[0], 8, edge))
-    copies_out[:, 8:16, :] = jnp.broadcast_to(rest[None], (copies_out.shape[0], 8, edge))
+    lines = [jnp.sum(jnp.where(eye, column, 0.0), axis=0, keepdims=True) for column in (peak, total)] + crosses
+    edge = rows // 2
+    tile_out[...] = jnp.concatenate([line[:, at : at + edge] for line in lines for at in (0, edge)], axis=0)
+
+
+def chosen_id(ids_ref, place, row, head):
+    lane = lax.broadcasted_iota(jnp.int32, place.shape, 1)
+    ids = jnp.where(head == 0, ids_ref[0:1, :], ids_ref[1:2, :])
+    return jnp.sum(jnp.where(lane == row, ids, 0.0), axis=1, keepdims=True)
+
+
+def student_kernel(side, core_ref, hidden_ref, head_ref, ids_ref, scores_out, lines_out):
+    rows, width = scores_out.shape
+    step = 32
+    for at in range(0, width, 256):
+        scores_out[:, at : at + 256] = jnp.dot(
+            hidden_ref[...], head_ref[:, at : at + 256], preferred_element_type=jnp.float32
+        )
+    lane = lax.broadcasted_iota(jnp.int32, (rows, rows), 1)
+    place = lax.broadcasted_iota(jnp.int32, (rows, rows), 0)
+    core = jnp.where(side == 0, core_ref[0], 1 - core_ref[0])
+    row, head = row_of(place, core)
+    ids = chosen_id(ids_ref, place, row, head)
+    columns = (lax.broadcasted_iota(jnp.int32, (step, width), 1) + core_ref[1]).astype(jnp.float32)
+    found = [[], [], [], []]
+    for at in range(0, rows, step):
+        scores = scores_out[at : at + step, :]
+        peak = jnp.max(scores, axis=1, keepdims=True)
+        power = jnp.exp((scores - peak) * 0.5)
+        found[0].append(peak)
+        found[1].append(jnp.sum(power * power, axis=1, keepdims=True))
+        found[2].append(jnp.sum(power, axis=1, keepdims=True))
+        found[3].append(jnp.sum(jnp.where(columns == ids[at : at + step], scores, 0.0), axis=1, keepdims=True))
+    eye = lane == place
+    lines = [jnp.sum(jnp.where(eye, jnp.concatenate(f, axis=0), 0.0), axis=0, keepdims=True) for f in found]
+    lines_out[...] = jnp.concatenate(lines + [jnp.zeros((4, rows), jnp.float32)], axis=0)
+
+
+def copy_kernel(core_ref, mine_ref, theirs_ref, stats_ref, copies_out):
+    mine, theirs = mine_ref[...], theirs_ref[...]
+    top = jnp.maximum(mine[0:2], theirs[0:2])
+    both = [jnp.exp(a[0:2] - top) for a in (mine, theirs)]
+    both = [jnp.concatenate([b, b, b, b], axis=0) for b in both]
+    tile = mine * both[0] + theirs * both[1]
+    tile = jnp.concatenate([top, tile[2:8]], axis=0)
+    rest = jnp.concatenate([stats_ref[...], jnp.zeros_like(stats_ref)], axis=0)
+    copies_out[:, 0:8, :] = jnp.broadcast_to(tile[None], copies_out[:, 0:8, :].shape)
+    copies_out[:, 8:16, :] = jnp.broadcast_to(rest[None], copies_out[:, 8:16, :].shape)
 
 
 def whole(shape):
@@ -127,19 +157,27 @@
     )(scalars, *operands)
 
 
-def teacher_sum(scalars, words, rows, width):
-    half = jax.ShapeDtypeStruct((rows, width), jnp.float32)
-    lines = jax.ShapeDtypeStruct((8, rows), jnp.float32)
+def teacher_sum(scalars, words, mine, theirs):
+    rows, width = mine.shape
     area = rows * width
+    tile = jax.ShapeDtypeStruct((8, rows // 2), jnp.float32)
+    half = jax.ShapeDtypeStruct(mine.shape, jnp.float32)
     scratch = [pltpu.VMEM((rows, width), jnp.float32)]
-    return call(teacher_kernel, scalars, (words,), (half, half, lines), 12, (12 * rows * area, 32 * area, area), scratch)
-
-
-def cross_terms(scalars, operands, devices):
-    lines, ids = operands[0], operands[-1]
-    copies = jax.ShapeDtypeStruct((devices, 16, lines.shape[1] // 2), jnp.float32)
-    area = operands[1].size
-    return call(cross_kernel, scalars, operands, (copies, jax.ShapeDtypeStruct(ids.shape, ids.dtype)), 9, (16 * area, 20 * area, 2 * area))
+    operands = (words, mine, theirs)
+    return call(teacher_kernel, scalars, operands, (half, half, tile), GRANT, (12 * rows * area, 40 * area, 3 * area), scratch)
+
+
+def student_half(side, scalars, hidden, head, ids):
+    rows, width = hidden.shape[0], head.shape[1]
+    area = rows * width
+    results = (jax.ShapeDtypeStruct((rows, width), jnp.float32), jax.ShapeDtypeStruct((8, rows), jnp.float32))
+    cost = (2 * area * hidden.shape[1], 4 * area + 2 * head.size, area)
+    return call(functools.partial(student_kernel, side), scalars, (hidden, head, ids), results, GRANT, cost)
+
+
+def chip_copies(scalars, mine, theirs, stats, chips):
+    copies = jax.ShapeDtypeStruct((chips, 16, mine.shape[1]), jnp.float32)
+    return call(copy_kernel, scalars, (mine, theirs, stats), (copies,), GRANT, (mine.size, 4 * copies.size, mine.size))[0]
 
 
 def slope_kernel(core_ref, shares_ref, ids_ref, mine_ref, theirs_ref, mine_t_ref, theirs_t_ref, mine_out, theirs_out, objective_out):
@@ -183,7 +221,7 @@
     place = lax.broadcasted_iota(jnp.int32, (rows, rows), 0)
     objective = [jnp.zeros((1, rows), jnp.float32), jnp.zeros((1, rows), jnp.float32)]
     base = core_ref[1]
-    columns = lax.broadcasted_iota(jnp.int32, (step, width), 1) + base
+    columns = (lax.broadcasted_iota(jnp.int32, (step, width), 1) + base).astype(jnp.float32)
     for side, scores, teacher, out in ((0, mine_ref, mine_t_ref, mine_out), (1, theirs_ref, theirs_t_ref, theirs_out)):
         first = (core_ref[0] == 0) == (side == 0)
         core = jnp.where(first, 0, 1)
@@ -204,7 +242,7 @@
         for k in (0, 1):
             inside = (lane == row) & (head == k)
             objective[k] = objective[k] + jnp.sum(jnp.where(inside, loss, 0.0), axis=0, keepdims=True)
-        ids = jnp.where(first, ids_ref[0], ids_ref[1])
+        ids = chosen_id(ids_ref, place, row, head)
         for at in range(0, rows, step):
             here = pl.ds(at, step)
             part = slice(at, at + step)
@@ -220,7 +258,7 @@
     half = jax.ShapeDtypeStruct(operands[2].shape, jnp.bfloat16)
     lines = jax.ShapeDtypeStruct((8, half.shape[0]), jnp.float32)
     area = operands[2].size
-    return call(slope_kernel, scalars, operands, (half, half, lines), 9, (40 * area, 24 * area, 6 * area))
+    return call(slope_kernel, scalars, operands, (half, half, lines), GRANT, (40 * area, 24 * area, 6 * area))
 
 
 def merge(parts):
@@ -255,7 +293,6 @@
 def local(teacher_hidden, teacher_head, student_hidden, student_head, target_ids):
     core = lax.axis_index("c")
     chips = lax.axis_size(WALK)
-    devices = lax.axis_size(EXCHANGE)
     stripes = teacher_head.shape[1]
     voc = teacher_head.shape[2]
     rows = teacher_hidden.shape[0]
@@ -274,45 +311,27 @@
     own = ring_gather(plane, "z")
     other = lax.ppermute(own, "c", pair)
 
-    order = target_ids.reshape(4, 4, 4, 2, 2, 2)
-    order = jnp.transpose(order, (3, 2, 1, 0, 5, 4)).reshape(2, rows, 1)
-    columns = lax.broadcasted_iota(jnp.int32, (1, voc), 1) + base
-
-    def student(hidden, side):
-        scores = jnp.dot(hidden, student_head, preferred_element_type=jnp.float32)
-        match = columns == jnp.where(side == 0, order[0], order[1])
-        top = jnp.max(scores, axis=1, keepdims=True)
-        powers = jnp.exp((scores - top) * 0.5)
-        stats = jnp.stack(
-            [
-                top[:, 0],
-                jnp.sum(powers * powers, axis=1),
-                jnp.sum(powers, axis=1),
-                jnp.sum(jnp.where(match, scores, 0.0), axis=1),
-            ]
-        )
-        return scores, stats
-
-    own_scores, own_stats = student(own, core)
-    other_scores, other_stats = student(other, 1 - core)
+    scalars = jnp.stack([core, base])
+    ids = target_ids.T.astype(jnp.float32)
+    own_scores, own_stats = student_half(0, scalars, own, student_head, ids)
+    other_scores, other_stats = student_half(1, scalars, other, student_head, ids)
+    own_stats, other_stats = own_stats[:4], other_stats[:4]
     stats = jnp.stack(
         [jnp.where(core == 0, own_stats, other_stats), jnp.where(core == 0, other_stats, own_stats)], axis=1
     ).reshape(4, 2 * rows)
-    stats = stats + 0.0 * words[0, 0, 0].astype(jnp.float32)
     around = [stats] + [lax.ppermute(stats, "z", [(i, (i + j) % 4) for i in range(4)]) for j in (1, 2, 3)]
     stats = merge(jnp.stack(around)).reshape(4, 4, rows // 2)
     stats = lax.dynamic_index_in_dim(stats, lax.axis_index("z"), 1, False)
-
-    scalars = jnp.stack([core, base])
-    own_teacher, other_teacher, lines = teacher_sum(scalars, words, rows, voc)
-    copies, order = cross_terms(
-        scalars, (lines, own_teacher, other_teacher, own_scores, other_scores, stats, order), devices
-    )
+    stats = stats + 0.0 * words[0, 0, 0].astype(jnp.float32)
+    stats = merge(jnp.stack([stats, lax.ppermute(stats, "c", pair)]))
+
+    own_teacher, other_teacher, tile = teacher_sum(scalars, words, own_scores, other_scores)
+    copies = chip_copies(scalars, tile, lax.ppermute(tile, "c", pair), stats, chips)
     hidden = jnp.concatenate([own, other], axis=0)
-    copies, hidden, order = lax.optimization_barrier((copies, hidden, order))
+    copies, hidden = lax.optimization_barrier((copies, hidden))
     shares = lax.all_to_all(copies, EXCHANGE, 0, 0, tiled=True)
     own_grad, other_grad, objective = slopes(
-        scalars, shares, order, own_scores, other_scores, own_teacher, other_teacher
+        scalars, shares, ids, own_scores, other_scores, own_teacher, other_teacher
     )
 
     contract = (((1,), (1,)), ((), ()))

time: 159 us -> 142 us (0.89)
  local copies, waits for them, and re-layouts: 36.1 us -> 23.4 us
  Pallas kernels: 6.57 us -> 14.1 us
  matrix products: 19.1 us -> 12.3 us
  blocking collectives: 55.1 us -> 51.8 us
  other arithmetic: 7.99 us -> 5.54 us
    pallas_call x3 -> x5, Pallas kernels: 6.57 us -> 14.1 us  [call(): pl.pallas_call(kernel, out_shape=tuple(results), grid_spec=pltpu.Prefetch...]
    dot_general x2 -> x0, matrix products: 6.77 us -> none  [student(): scores = jnp.dot(hidden, student_head, preferred_element_type=jnp.float32)]
    select_n x4 -> x0, local copies, waits for them, and re-layouts: 4.15 us -> none  [student(): match = columns == jnp.where(side == 0, order[0], order[1])]
    all_to_all x1, blocking collectives: 28.6 us -> 24.9 us  [local(): shares = lax.all_to_all(copies, EXCHANGE, 0, 0, tiled=True)]
    unnamed x34 -> x23, local copies, waits for them, and re-layouts: 10.3 us -> 6.82 us
    reshape x2 -> x0, local copies, waits for them, and re-layouts: 2.68 us -> none  [the longest x1 1.82 us: local(): order = jnp.transpose(order, (3, 2, 1, 0, 5, 4)).reshape(2, rows, 1)]
    select_n x3 -> x0, other arithmetic: 1.75 us -> none  [the longest x1 1.73 us: student(): match = columns == jnp.where(side == 0, order[0], order[1])]
    transpose x1 -> x0, local copies, waits for them, and re-layouts: 1.64 us -> none  [local(): order = jnp.transpose(order, (3, 2, 1, 0, 5, 4)).reshape(2, rows, 1)]
  transfers between devices with their start and end apart: 10 -> 12, of which waited for: 4 -> 6; matrix products, arithmetic and copies ran while one was open for 30% -> 20% of each run, Pallas kernels for 2% -> 8%
where the time goes in v1:
time: 142 us
  blocking collectives  51.8 us (36%)
  starting transfers between devices  24.9 us (18%)
  local copies, waits for them, and re-layouts  23.4 us (16%)
  Pallas kernels  14.1 us (10%)
  matrix products  12.3 us (9%)
  waiting for transfers between devices  7.99 us (6%)
  other arithmetic  5.54 us (4%)
  between operations  1.57 us (1%)
    all_to_all x1, blocking collectives, local(): share = lax.all_to_all(share, WALK, 0, 0, tiled=True)  26.9 us
    all_to_all x1, blocking collectives, local(): shares = lax.all_to_all(copies, EXCHANGE, 0, 0, tiled=True)  24.9 us
    pallas_call x5, Pallas kernels, call(): pl.pallas_call(kernel, out_shape=tuple(results), grid_spec=pltpu.Prefetch...  14.1 us
    all_to_all x1, starting transfers between devices, everywhere(): return lax.all_to_all(copies, axes, 0, 0, tiled=True)  7.16 us
    unnamed x23, local copies, waits for them, and re-layouts  6.82 us
    all_to_all x1, starting transfers between devices, local(): words = lax.all_to_all(words, STRIPES, 0, 0, tiled=True)  6.67 us
    ppermute x3, waiting for transfers between devices, ring_gather(): lax.ppermute(block, axes, [(i, (i + step) % size) for i in range(size)])  6.55 us
    ppermute x3, starting transfers between devices, ring_gather(): lax.ppermute(block, axes, [(i, (i + step) % size) for i in range(size)])  6.5 us
  transfers between devices with their start and end apart: 12, of which 6 were waited for; matrix products, arithmetic and copies ran while one was open for 20% of the time, Pallas kernels for 8%

profile of v1, /device:TPU:0, one launch (start us, length us, event | category | flops | bytes accessed | tf_op | source)
XLA Modules:
  0.0 141.6 jit_solution(11358265576227691157)
XLA Ops:
  2.3 7.2 %all-to-all-start.1 = ((bf16[16,4,2560]{2,1,0:T(4,128)(2,1)}), bf16[16,4,2560]{2,1,0:T(4,128)(2,1)}, u32[]{:S(2)}, u32[]{:S(2)}) async-start(bf16[16,4,2560]{2,1,0:T(4,128)(2,1)} %broadcast_in_dim.24), calls=%async_computation.1 | async-start | bytes 655360 | tf_op jit(solution)/shard_map/all_to_all | solution.py:290
  9.5 5.7 %abs_reduce_fusion = (f32[8,256]{1,0:T(8,128)S(1)}, f32[8,768,256]{1,2,0:T(8,128)S(1)}) fusion(bf16[512,8,768]{2,1,0:T(8,128)(2,1)} %param.8, bf16[256,512]{1,0:T(8,128)(2,1)S(1)} %copy-done), kind=kOutput, calls=%fused_computation.3 | convolution fusion | flops 1613756416 | bytes 12853248 | tf_op jit(solution)/shard_map/rd,dsv->srv/dot_general | solution.py:303
  16.6 1.9 %copy.30 = s32[2,2,2,264,384]{4,3,0,1,2:T(8,128)} copy(s32[2,2,2,264,384]{4,3,2,1,0:T(8,128)S(1)} %bitcast.95) | data formatting | bytes 6488064 | tf_op jit(solution)/shard_map/reshape | solution.py:305
  18.9 6.7 %all-to-all-start = ((s32[8,264,384]{2,1,0:T(8,128)}), s32[8,264,384]{2,1,0:T(8,128)S(1)}, u32[]{:S(2)}, u32[]{:S(2)}) async-start(s32[8,264,384]{2,1,0:T(8,128)} %bitcast.94), calls=%async_computation | async-start | bytes 6488064 | tf_op jit(solution)/shard_map/all_to_all | solution.py:306
  25.6 1.8 %reshape.127 = bf16[64,2560]{1,0:T(8,128)(2,1)} reshape(bf16[16,4,2560]{2,1,0:T(4,128)(2,1)} %all-to-all-done.1) | data formatting | bytes 655360 | tf_op jit(solution)/shard_map/reshape | solution.py:309
  27.4 1.9 %collective-permute-start = (bf16[64,2560]{1,0:T(8,128)(2,1)}, bf16[64,2560]{1,0:T(8,128)(2,1)}, u32[]{:S(2)}, u32[]{:S(2)}) collective-permute-start(bf16[64,2560]{1,0:T(8,128)(2,1)} %reshape.127), channel_id=1, source_target_pairs={{0,2},{2,4},{4,6},{6,0},{1,3},{3,5},{5,7},{7,1},{8,10},{10,12},{12... | collective-permute-start | bytes 983048 | tf_op jit(solution)/shard_map/ppermute | solution.py:283
  29.3 3.6 %collective-permute-start.1 = (bf16[64,2560]{1,0:T(8,128)(2,1)}, bf16[64,2560]{1,0:T(8,128)(2,1)}, u32[]{:S(2)}, u32[]{:S(2)}) collective-permute-start(bf16[64,2560]{1,0:T(8,128)(2,1)} %reshape.127), channel_id=1, source_target_pairs={{0,4},{2,6},{4,0},{6,2},{1,5},{3,7},{5,1},{7,3},{8,12},{10,14},{12... | collective-permute-start | bytes 983048 | tf_op jit(solution)/shard_map/ppermute | solution.py:283
  32.9 1.0 collective-permute-start.2
  33.9 1.8 %broadcast_in_dim.25 = bf16[1,64,2560]{2,1,0:T(8,128)(2,1)} reshape(bf16[16,4,2560]{2,1,0:T(4,128)(2,1)} %all-to-all-done.1) | data formatting | bytes 655360 | tf_op jit(solution)/shard_map/jit(dynamic_update_index_in_dim)/broadcast_in_dim | solution.py:281
  35.7 1.1 broadcast_in_dim.23
  36.8 1.7 %constant_dynamic-update-slice_fusion = bf16[4,64,2560]{2,1,0:T(8,128)(2,1)} fusion(bf16[4,64,2560]{2,1,0:T(8,128)(2,1)} %broadcast_in_dim.23, bf16[1,64,2560]{2,1,0:T(8,128)(2,1)} %broadcast_in_dim.25, s32[]{:T(128)S(6)} %select_n.42), kind=kLoop, calls=%fused_computation.53 | loop fusion | bytes 655364 | tf_op jit(solution)/shard_map/jit(dynamic_update_index_in_dim)/dynamic_update_slice | solution.py:281
  38.5 0.9 collective-permute-done
  39.4 1.7 %bitcast_dynamic-update-slice_fusion.2 = bf16[4,64,2560]{2,1,0:T(8,128)(2,1)} fusion(bf16[4,64,2560]{2,1,0:T(8,128)(2,1)} %constant_dynamic-update-slice_fusion, s32[]{:T(128)S(6)} %select_n.44, bf16[64,2560]{1,0:T(8,128)(2,1)} %collective-permute-done), kind=kLoop, calls=%fused_computation.17 | loop fusion | bytes 655364 | tf_op jit(solution)/shard_map/jit(dynamic_update_index_in_dim)/dynamic_update_slice | solution.py:284
  41.2 5.6 %collective-permute-done.1 = bf16[64,2560]{1,0:T(8,128)(2,1)} collective-permute-done((bf16[64,2560]{1,0:T(8,128)(2,1)}, bf16[64,2560]{1,0:T(8,128)(2,1)}, u32[]{:S(2)}, u32[]{:S(2)}) %collective-permute-start.1) | collective-permute-done | bytes 327712 | tf_op jit(solution)/shard_map/ppermute | solution.py:283
  46.8 1.7 %bitcast_dynamic-update-slice_fusion.1 = bf16[4,64,2560]{2,1,0:T(8,128)(2,1)} fusion(bf16[4,64,2560]{2,1,0:T(8,128)(2,1)} %bitcast_dynamic-update-slice_fusion.2, s32[]{:T(128)S(6)} %select_n.46, bf16[64,2560]{1,0:T(8,128)(2,1)} %collective-permute-done.1), kind=kLoop, calls=%fused_computation.16 | loop fusion | bytes 655364 | tf_op jit(solution)/shard_map/jit(dynamic_update_index_in_dim)/dynamic_update_slice | solution.py:284
  48.5 1.7 %bitcast_dynamic-update-slice_fusion = bf16[4,64,2560]{2,1,0:T(8,128)(2,1)} fusion(bf16[4,64,2560]{2,1,0:T(8,128)(2,1)} %bitcast_dynamic-update-slice_fusion.1, s32[]{:T(128)S(6)} %select_n.48, bf16[64,2560]{1,0:T(8,128)(2,1)} %collective-permute-done.2), kind=kLoop, calls=%fused_computation.15 | loop fusion | bytes 655364 | tf_op jit(solution)/shard_map/jit(dynamic_update_index_in_dim)/dynamic_update_slice | solution.py:284
  50.3 2.1 %copy-done.1 = bf16[2560,768]{1,0:T(8,128)(2,1)S(1)} copy-done((bf16[2560,768]{1,0:T(8,128)(2,1)S(1)}, bf16[2560,768]{1,0:T(8,128)(2,1)}, u32[]{:S(2)}) %copy-start.1) | copy-done | bytes 3932184
  52.4 4.1 %shard_map.76 = (f32[256,768]{1,0:T(8,128)S(1)}, f32[8,256]{1,0:T(8,128)S(1)}) custom-call(s32[2]{0:T(128)S(1)} %pad_add_fusion.1.core_ref, bf16[256,2560]{1,0:T(8,128)(2,1)} %bitcast.11.hidden_ref, bf16[2560,768]{1,0:T(8,128)(2,1)S(1)} %copy-done.1, f32[2,256]{1,0:T(2,128)S(1)} %convert_bitcast_fusion.1.ids_ref), custom_call_target="tpu_custom_call" | custom-call | flops 1006632960 | bytes 4718592 | tf_op jit(solution)/shard_map/pallas_call | solution.py:145
  56.5 0.9 copy-done.4
  57.4 3.8 %shard_map.77 = (f32[256,768]{1,0:T(8,128)S(1)}, f32[8,256]{1,0:T(8,128)S(1)}) custom-call(s32[2]{0:T(128)S(1)} %pad_add_fusion.1.core_ref, bf16[256,2560]{1,0:T(8,128)(2,1)} %collective-permute-done.3.hidden_ref, bf16[2560,768]{1,0:T(8,128)(2,1)S(1)} %copy-done.2, f32[2,256]{1,0:T(2,128)S(1)} %convert_bitcast_fusion.1.ids_ref), custom_call_target="tpu_custom_call" | custom-call | flops 1006632960 | bytes 4718592 | tf_op jit(solution)/shard_map/pallas_call | solution.py:145
  62.6 1.9 %collective-permute-start.6 = (f32[4,512]{1,0:T(4,128)S(1)}, f32[4,512]{1,0:T(4,128)S(1)}, u32[]{:S(2)}, u32[]{:S(2)}) collective-permute-start(f32[4,512]{1,0:T(4,128)S(1)} %bitcast.98), channel_id=1, source_target_pairs={{0,4},{2,6},{4,0},{6,2},{1,5},{3,7},{5,1},{7,3},{8,12},{10,14},{12... | collective-permute-start | bytes 24584 | tf_op jit(solution)/shard_map/ppermute | solution.py:322
  64.4 1.3 collective-permute-start.5
  65.8 3.4 %pad_maximum_fusion = bf16[512,2560]{1,0:T(8,128)(2,1)} fusion(bf16[256,2560]{1,0:T(8,128)(2,1)} %collective-permute-done.3.hidden_ref, bf16[256,2560]{1,0:T(8,128)(2,1)} %bitcast.11.hidden_ref), kind=kLoop, calls=%fused_computation.11 | loop fusion | flops 5242880 | bytes 5242880 | tf_op jit(solution)/shard_map/concatenate | solution.py:330
  70.9 1.1 copy-done.5
  72.0 1.1 copy-done.8
  73.1 3.3 %shard_map.78 = (f32[256,768]{1,0:T(8,128)S(1)}, f32[256,768]{1,0:T(8,128)S(1)}, f32[8,128]{1,0:T(8,128)S(1)}) custom-call(s32[2]{0:T(128)S(1)} %pad_add_fusion.1.core_ref, s32[8,264,384]{2,1,0:T(8,128)S(1)} %all-to-all-done.words_ref, f32[256,768]{1,0:T(8,128)S(1)} %copy-done.5, f32[256,768]{1,0:T(8,128)S(1)} %copy-done.8), custom_call_target="tpu_custom_call" | custom-call | flops 603979776 | bytes 7864320 | tf_op jit(solution)/shard_map/pallas_call | solution.py:145
  78.4 24.9 %all_to_all.20.shares_ref = f32[64,16,128]{2,1,0:T(8,128)S(1)} all-to-all(f32[64,16,128]{2,1,0:T(8,128)S(1)} %shard_map.79), channel_id=1, replica_groups=mesh['xh'=2,'xl'=2,'yh'=2,'yl'=2,'z'=4,'c'=2] {'z','yh','xh','yl','xl'}, dimensions={0} | all-to-all | bytes 1048576 | tf_op jit(solution)/shard_map/all_to_all | solution.py:332
  103.3 2.4 %shard_map.80 = (bf16[256,768]{1,0:T(8,128)(2,1)S(1)}, bf16[256,768]{1,0:T(8,128)(2,1)S(1)}, f32[8,256]{1,0:T(8,128)S(1)}) custom-call(s32[2]{0:T(128)S(1)} %pad_add_fusion.1.core_ref, f32[64,16,128]{2,1,0:T(8,128)S(1)} %all_to_all.20.shares_ref, f32[2,256]{1,0:T(2,128)S(1)} %convert_bitcast_fusion.1.ids_ref, f32[256,768]{1,0:T(8,128)S(1)} %copy-done.6, ...), custom_call_target="tpu_custom_call" | custom-call | flops 7864320 | bytes 4718592 | tf_op jit(solution)/shard_map/pallas_call | solution.py:145
  105.7 1.2 fusion.31
  107.6 4.2 %convolution_convert_fusion = bf16[2560,768]{1,0:T(8,128)(2,1)} fusion(bf16[512,2560]{1,0:T(8,128)(2,1)S(1)} %copy-done.9, bf16[256,768]{1,0:T(8,128)(2,1)S(1)} %get-tuple-element.39, bf16[256,768]{1,0:T(8,128)(2,1)S(1)} %get-tuple-element.38), kind=kOutput, calls=%fused_computation.4 | convolution fusion | flops 2016804864 | bytes 7340032 | tf_op jit(solution)/shard_map/dot_general | solution.py:342
  111.9 1.2 fusion.2
  113.5 26.9 %all_to_all.21 = bf16[64,4,2560]{2,1,0:T(4,128)(2,1)S(1)} all-to-all(bf16[64,4,2560]{2,1,0:T(4,128)(2,1)S(1)} %reshape.130), channel_id=1, replica_groups=mesh['xh'=2,'xl'=2,'yh'=2,'yl'=2,'z'=4,'c'=2] {'z','yh','yl','xh','xl'}, dimensions={0} | all-to-all | bytes 2621440 | tf_op jit(solution)/shard_map/all_to_all | solution.py:349
  (59 shorter events, 10.1 us)
Async XLA Ops:
  0.6 8.8 %copy-start = (bf16[256,512]{1,0:T(8,128)(2,1)S(1)}, bf16[256,512]{1,0:T(8,128)(2,1)}, u32[]{:S(2)}) copy-start(bf16[256,512]{1,0:T(8,128)(2,1)} %param.7) | copy-start | bytes 786436
  2.3 16.6 %all-to-all-start.1 = ((bf16[16,4,2560]{2,1,0:T(4,128)(2,1)}), bf16[16,4,2560]{2,1,0:T(4,128)(2,1)}, u32[]{:S(2)}, u32[]{:S(2)}) async-start(bf16[16,4,2560]{2,1,0:T(4,128)(2,1)} %broadcast_in_dim.24), calls=%async_computation.1 | async-start | bytes 655360 | tf_op jit(solution)/shard_map/all_to_all | solution.py:290
  18.9 50.5 %all-to-all-start = ((s32[8,264,384]{2,1,0:T(8,128)}), s32[8,264,384]{2,1,0:T(8,128)S(1)}, u32[]{:S(2)}, u32[]{:S(2)}) async-start(s32[8,264,384]{2,1,0:T(8,128)} %bitcast.94), calls=%async_computation | async-start | bytes 6488064 | tf_op jit(solution)/shard_map/all_to_all | solution.py:306
  25.6 24.7 %copy-start.10 = (s32[256,2]{0,1:T(2,128)S(1)}, s32[256,2]{0,1:T(2,128)}, u32[]{:S(2)}) copy-start(s32[256,2]{0,1:T(2,128)} %param.11) | copy-start | bytes 6148
  27.4 12.1 %collective-permute-start = (bf16[64,2560]{1,0:T(8,128)(2,1)}, bf16[64,2560]{1,0:T(8,128)(2,1)}, u32[]{:S(2)}, u32[]{:S(2)}) collective-permute-start(bf16[64,2560]{1,0:T(8,128)(2,1)} %reshape.127), channel_id=1, source_target_pairs={{0,2},{2,4},{4,6},{6,0},{1,3},{3,5},{5,7},{7,1},{8,10},{10,12},{12... | collective-permute-start | bytes 983048 | tf_op jit(solution)/shard_map/ppermute | solution.py:283
  29.3 17.5 %collective-permute-start.1 = (bf16[64,2560]{1,0:T(8,128)(2,1)}, bf16[64,2560]{1,0:T(8,128)(2,1)}, u32[]{:S(2)}, u32[]{:S(2)}) collective-permute-start(bf16[64,2560]{1,0:T(8,128)(2,1)} %reshape.127), channel_id=1, source_target_pairs={{0,4},{2,6},{4,0},{6,2},{1,5},{3,7},{5,1},{7,3},{8,12},{10,14},{12... | collective-permute-start | bytes 983048 | tf_op jit(solution)/shard_map/ppermute | solution.py:283
  32.9 15.6 %collective-permute-start.2 = (bf16[64,2560]{1,0:T(8,128)(2,1)}, bf16[64,2560]{1,0:T(8,128)(2,1)}, u32[]{:S(2)}, u32[]{:S(2)}) collective-permute-start(bf16[64,2560]{1,0:T(8,128)(2,1)} %reshape.127), channel_id=1, source_target_pairs={{0,6},{2,0},{4,2},{6,4},{1,7},{3,1},{5,3},{7,5},{8,14},{10,8},{12,... | collective-permute-start | bytes 983048 | tf_op jit(solution)/shard_map/ppermute | solution.py:283
  50.2 7.2 %collective-permute-start.3 = (bf16[256,2560]{1,0:T(8,128)(2,1)}, bf16[256,2560]{1,0:T(8,128)(2,1)}, u32[]{:S(2)}, u32[]{:S(2)}) collective-permute-start(bf16[256,2560]{1,0:T(8,128)(2,1)} %bitcast.11.hidden_ref), channel_id=1, source_target_pairs={{0,1},{1,0},{2,3},{3,2},{4,5},{5,4},{6,7},{7,6},{8,9},{9,8},{10,11... | collective-permute-start | bytes 3932168 | tf_op jit(solution)/shard_map/ppermute | solution.py:312
  50.3 2.1 %copy-start.1 = (bf16[2560,768]{1,0:T(8,128)(2,1)S(1)}, bf16[2560,768]{1,0:T(8,128)(2,1)}, u32[]{:S(2)}) copy-start(bf16[2560,768]{1,0:T(8,128)(2,1)} %head_ref.3) | copy-start | bytes 11796484
  52.4 5.0 %copy-start.2 = (bf16[2560,768]{1,0:T(8,128)(2,1)S(1)}, bf16[2560,768]{1,0:T(8,128)(2,1)}, u32[]{:S(2)}) copy-start(bf16[2560,768]{1,0:T(8,128)(2,1)} %head_ref.3) | copy-start | bytes 11796484
  56.5 0.9 copy-start.4
  61.2 0.9 copy-start.7
  62.1 7.0 %collective-permute-start.7 = (f32[4,512]{1,0:T(4,128)S(1)}, f32[4,512]{1,0:T(4,128)S(1)}, u32[]{:S(2)}, u32[]{:S(2)}) collective-permute-start(f32[4,512]{1,0:T(4,128)S(1)} %bitcast.97), channel_id=1, source_target_pairs={{0,6},{2,0},{4,2},{6,4},{1,7},{3,1},{5,3},{7,5},{8,14},{10,8},{12,... | collective-permute-start | bytes 24584 | tf_op jit(solution)/shard_map/ppermute | solution.py:322
  62.6 6.6 %collective-permute-start.6 = (f32[4,512]{1,0:T(4,128)S(1)}, f32[4,512]{1,0:T(4,128)S(1)}, u32[]{:S(2)}, u32[]{:S(2)}) collective-permute-start(f32[4,512]{1,0:T(4,128)S(1)} %bitcast.98), channel_id=1, source_target_pairs={{0,4},{2,6},{4,0},{6,2},{1,5},{3,7},{5,1},{7,3},{8,12},{10,14},{12... | collective-permute-start | bytes 24584 | tf_op jit(solution)/shard_map/ppermute | solution.py:322
  64.4 4.9 %collective-permute-start.5 = (f32[4,512]{1,0:T(4,128)S(1)}, f32[4,512]{1,0:T(4,128)S(1)}, u32[]{:S(2)}, u32[]{:S(2)}) collective-permute-start(f32[4,512]{1,0:T(4,128)S(1)} %bitcast.99), channel_id=1, source_target_pairs={{0,2},{2,4},{4,6},{6,0},{1,3},{3,5},{5,7},{7,1},{8,10},{10,12},{12... | collective-permute-start | bytes 24584 | tf_op jit(solution)/shard_map/ppermute | solution.py:322
  70.6 6.5 %collective-permute-start.8 = (f32[4,128]{1,0:T(4,128)S(1)}, f32[4,128]{1,0:T(4,128)S(1)}, u32[]{:S(2)}, u32[]{:S(2)}) collective-permute-start(f32[4,128]{1,0:T(4,128)S(1)} %bitcast.102), channel_id=1, source_target_pairs={{0,1},{1,0},{2,3},{3,2},{4,5},{5,4},{6,7},{7,6},{8,9},{9,8},{10,11... | collective-permute-start | bytes 6152 | tf_op jit(solution)/shard_map/ppermute | solution.py:326
  70.9 1.1 copy-start.5
  72.0 1.1 copy-start.8
  73.1 30.2 %copy-start.6 = (f32[256,768]{1,0:T(8,128)S(1)}, f32[256,768]{1,0:T(8,128)}, u32[]{:S(2)}) copy-start(f32[256,768]{1,0:T(8,128)} %copy-done.4) | copy-start | bytes 2359300
  76.5 29.3 %copy-start.3 = (bf16[2560,768]{1,0:T(8,128)(2,1)S(1)}, bf16[2560,768]{1,0:T(8,128)(2,1)}, u32[]{:S(2)}) copy-start(bf16[2560,768]{1,0:T(8,128)(2,1)} %head_ref.3) | copy-start | bytes 11796484
  76.5 1.4 collective-permute-start.4
  105.7 1.9 %copy-start.9 = (bf16[512,2560]{1,0:T(8,128)(2,1)S(1)}, bf16[512,2560]{1,0:T(8,128)(2,1)}, u32[]{:S(2)}) copy-start(bf16[512,2560]{1,0:T(8,128)(2,1)} %pad_maximum_fusion) | copy-start | bytes 7864324
  106.9 5.0 %collective-permute-start.9 = (f32[256,2560]{1,0:T(8,128)S(1)}, f32[256,2560]{1,0:T(8,128)S(1)}, u32[]{:S(2)}, u32[]{:S(2)}) collective-permute-start(f32[256,2560]{1,0:T(8,128)S(1)} %fusion.31), channel_id=1, source_target_pairs={{0,1},{1,0},{2,3},{3,2},{4,5},{5,4},{6,7},{7,6},{8,9},{9,8},{10,11... | collective-permute-start | bytes 7864328 | tf_op jit(solution)/shard_map/ppermute | solution.py:339

commit v2 on v1

--- a/solution.py
+++ b/solution.py
@@ -274,15 +274,44 @@
     )
 
 
-def ring_gather(block, axes):
-    size = lax.axis_size(axes)
-    here = lax.axis_index(axes)
-    whole = jnp.zeros((size,) + block.shape, block.dtype)
-    whole = lax.dynamic_update_index_in_dim(whole, block, here, 0)
+def place_kernel(count, places_ref, *refs):
+    blocks, out_ref, sems = refs[:count], refs[count], refs[count + 1]
+    rows = blocks[0].shape[0]
+    copies = []
+    for i, block in enumerate(blocks):
+        at = pl.multiple_of(places_ref[i] * rows, rows)
+        copies.append(pltpu.make_async_copy(block, out_ref.at[pl.ds(at, rows), :], sems.at[i]))
+    for copy in copies:
+        copy.start()
+    for copy in copies:
+        copy.wait()
+
+
+def place_blocks(places, *blocks):
+    count = len(blocks)
+    rows, width = blocks[0].shape
+    return pl.pallas_call(
+        functools.partial(place_kernel, count),
+        out_shape=jax.ShapeDtypeStruct((count * rows, width), blocks[0].dtype),
+        grid_spec=pltpu.PrefetchScalarGridSpec(
+            num_scalar_prefetch=1,
+            grid=(1,),
+            in_specs=[pl.BlockSpec(memory_space=pl.ANY)] * count,
+            out_specs=pl.BlockSpec(memory_space=pl.ANY),
+            scratch_shapes=[pltpu.SemaphoreType.DMA((count,))],
+        ),
+        compiler_params=pltpu.CompilerParams(vmem_limit_bytes=2 << 20),
+        cost_estimate=pl.CostEstimate(flops=0, bytes_accessed=2 * count * blocks[0].size * 2, transcendentals=0),
+    )(places, *blocks)
+
+
+def ring_gather(block, axis):
+    size = lax.axis_size(axis)
+    here = lax.axis_index(axis)
+    blocks = [block]
     for step in range(1, size):
-        taken = lax.ppermute(block, axes, [(i, (i + step) % size) for i in range(size)])
-        whole = lax.dynamic_update_index_in_dim(whole, taken, (here + size - step) % size, 0)
-    return whole.reshape((size * block.shape[0],) + block.shape[1:])
+        blocks.append(lax.ppermute(block, axis, [(i, (i + step) % size) for i in range(size)]))
+    return place_blocks((here + size - jnp.arange(size, dtype=jnp.int32)) % size, *blocks)
 
 
 def everywhere(value, axes, count):
@@ -327,7 +356,7 @@
 
     own_teacher, other_teacher, tile = teacher_sum(scalars, words, own_scores, other_scores)
     copies = chip_copies(scalars, tile, lax.ppermute(tile, "c", pair), stats, chips)
-    hidden = jnp.concatenate([own, other], axis=0)
+    hidden = place_blocks(jnp.arange(2, dtype=jnp.int32), own, other)
     copies, hidden = lax.optimization_barrier((copies, hidden))
     shares = lax.all_to_all(copies, EXCHANGE, 0, 0, tiled=True)
     own_grad, other_grad, objective = slopes(

time: 142 us -> 170 us (1.20)
  Pallas kernels: 14.1 us -> 47.9 us
  local copies, waits for them, and re-layouts: 23.4 us -> 16 us
  waiting for transfers between devices: 7.99 us -> 14.9 us
  other arithmetic: 5.54 us -> 2.15 us
  blocking collectives: 51.8 us -> 50 us
    pallas_call x0 -> x2, Pallas kernels: none -> 33.7 us  [place_blocks(): pl.pallas_call(functools.partial(place_kernel, count), out_shape=jax.Shap...]
    dynamic_update_slice x4 -> x0, local copies, waits for them, and re-layouts: 6.87 us -> none  [the longest x3 5.16 us: ring_gather(): lax.dynamic_update_index_in_dim(whole, taken, (here + size - step) % size...]
    ppermute x3, waiting for transfers between devices: 6.55 us -> 12.9 us  [ring_gather(): lax.ppermute(block, axis, [(i, (i + step) % size) for i in range(size)])]
    concatenate x1 -> x0, other arithmetic: 3.4 us -> none  [local(): hidden = jnp.concatenate([own, other], axis=0)]
    broadcast_in_dim x2 -> x0, local copies, waits for them, and re-layouts: 2.94 us -> none  [the longest x1 1.79 us: ring_gather(): whole = lax.dynamic_update_index_in_dim(whole, block, here, 0)]
    unnamed x23 -> x27, local copies, waits for them, and re-layouts: 6.82 us -> 9.28 us
    all_to_all x1, blocking collectives: 24.9 us -> 23.1 us  [local(): shares = lax.all_to_all(copies, EXCHANGE, 0, 0, tiled=True)]
  transfers between devices with their start and end apart: 12 -> 12, of which waited for: 6 -> 6; matrix products, arithmetic and copies ran while one was open for 20% -> 9% of each run, Pallas kernels for 8% -> 26%
where the time goes in v2:
time: 170 us
  blocking collectives  50 us (29%)
  Pallas kernels  47.9 us (28%)
  starting transfers between devices  25 us (15%)
  local copies, waits for them, and re-layouts  16 us (9%)
  waiting for transfers between devices  14.9 us (9%)
  matrix products  12.3 us (7%)
  other arithmetic  2.15 us (1%)
    pallas_call x2, Pallas kernels, place_blocks(): pl.pallas_call(functools.partial(place_kernel, count), out_shape=jax.Shap...  33.7 us
    all_to_all x1, blocking collectives, local(): share = lax.all_to_all(share, WALK, 0, 0, tiled=True)  26.9 us
    all_to_all x1, blocking collectives, local(): shares = lax.all_to_all(copies, EXCHANGE, 0, 0, tiled=True)  23.1 us
    pallas_call x5, Pallas kernels, call(): pl.pallas_call(kernel, out_shape=tuple(results), grid_spec=pltpu.Prefetch...  14.2 us
    ppermute x3, waiting for transfers between devices, ring_gather(): lax.ppermute(block, axis, [(i, (i + step) % size) for i in range(size)])  12.9 us
    unnamed x27, local copies, waits for them, and re-layouts  9.28 us
    all_to_all x1, starting transfers between devices, everywhere(): return lax.all_to_all(copies, axes, 0, 0, tiled=True)  7.16 us
    all_to_all x1, starting transfers between devices, local(): words = lax.all_to_all(words, STRIPES, 0, 0, tiled=True)  6.61 us
  transfers between devices with their start and end apart: 12, of which 6 were waited for; matrix products, arithmetic and copies ran while one was open for 9% of the time, Pallas kernels for 26%

profile of v2, /device:TPU:0, one launch (start us, length us, event | category | flops | bytes accessed | tf_op | source)
XLA Modules:
  0.0 169.8 jit_solution(1220696114436148568)
XLA Ops:
  1.5 0.8 broadcast_in_dim.2
  2.3 7.2 %all-to-all-start.1 = ((bf16[16,4,2560]{2,1,0:T(4,128)(2,1)}), bf16[16,4,2560]{2,1,0:T(4,128)(2,1)}, u32[]{:S(2)}, u32[]{:S(2)}) async-start(bf16[16,4,2560]{2,1,0:T(4,128)(2,1)} %broadcast_in_dim.2), calls=%async_computation.1 | async-start | bytes 655360 | tf_op jit(solution)/shard_map/all_to_all | solution.py:319
  9.4 5.7 %abs_reduce_fusion = (f32[8,256]{1,0:T(8,128)S(1)}, f32[8,768,256]{1,2,0:T(8,128)S(1)}) fusion(bf16[512,8,768]{2,1,0:T(8,128)(2,1)} %param.8, bf16[256,512]{1,0:T(8,128)(2,1)S(1)} %copy-done), kind=kOutput, calls=%fused_computation.3 | convolution fusion | flops 1613756416 | bytes 12853248 | tf_op jit(solution)/shard_map/rd,dsv->srv/dot_general | solution.py:332
  15.2 0.8 convert_bitcast_fusion
  16.5 1.9 %copy.30 = s32[2,2,2,264,384]{4,3,0,1,2:T(8,128)} copy(s32[2,2,2,264,384]{4,3,2,1,0:T(8,128)S(1)} %bitcast.88) | data formatting | bytes 6488064 | tf_op jit(solution)/shard_map/reshape | solution.py:334
  18.9 6.6 %all-to-all-start = ((s32[8,264,384]{2,1,0:T(8,128)}), s32[8,264,384]{2,1,0:T(8,128)S(1)}, u32[]{:S(2)}, u32[]{:S(2)}) async-start(s32[8,264,384]{2,1,0:T(8,128)} %bitcast.87), calls=%async_computation | async-start | bytes 6488064 | tf_op jit(solution)/shard_map/all_to_all | solution.py:335
  25.5 1.8 %reshape.123.refs_0_ = bf16[64,2560]{1,0:T(8,128)(2,1)} reshape(bf16[16,4,2560]{2,1,0:T(4,128)(2,1)} %all-to-all-done.1) | data formatting | bytes 655360 | tf_op jit(solution)/shard_map/reshape | solution.py:338
  27.3 1.9 %collective-permute-start = (bf16[64,2560]{1,0:T(8,128)(2,1)}, bf16[64,2560]{1,0:T(8,128)(2,1)}, u32[]{:S(2)}, u32[]{:S(2)}) collective-permute-start(bf16[64,2560]{1,0:T(8,128)(2,1)} %reshape.123.refs_0_), channel_id=1, source_target_pairs={{0,2},{2,4},{4,6},{6,0},{1,3},{3,5},{5,7},{7,1},{8,10},{10,12},{12... | collective-permute-start | bytes 983048 | tf_op jit(solution)/shard_map/ppermute | solution.py:313
  29.2 3.6 %collective-permute-start.1 = (bf16[64,2560]{1,0:T(8,128)(2,1)}, bf16[64,2560]{1,0:T(8,128)(2,1)}, u32[]{:S(2)}, u32[]{:S(2)}) collective-permute-start(bf16[64,2560]{1,0:T(8,128)(2,1)} %reshape.123.refs_0_), channel_id=1, source_target_pairs={{0,4},{2,6},{4,0},{6,2},{1,5},{3,7},{5,1},{7,3},{8,12},{10,14},{12... | collective-permute-start | bytes 983048 | tf_op jit(solution)/shard_map/ppermute | solution.py:313
  32.8 1.0 collective-permute-start.2
  33.8 5.5 %collective-permute-done.refs_1_ = bf16[64,2560]{1,0:T(8,128)(2,1)} collective-permute-done((bf16[64,2560]{1,0:T(8,128)(2,1)}, bf16[64,2560]{1,0:T(8,128)(2,1)}, u32[]{:S(2)}, u32[]{:S(2)}) %collective-permute-start) | collective-permute-done | bytes 327712 | tf_op jit(solution)/shard_map/ppermute | solution.py:313
  39.4 7.4 %collective-permute-done.1.refs_2_ = bf16[64,2560]{1,0:T(8,128)(2,1)} collective-permute-done((bf16[64,2560]{1,0:T(8,128)(2,1)}, bf16[64,2560]{1,0:T(8,128)(2,1)}, u32[]{:S(2)}, u32[]{:S(2)}) %collective-permute-start.1) | collective-permute-done | bytes 327712 | tf_op jit(solution)/shard_map/ppermute | solution.py:313
  46.7 1.0 copy-done.11
  47.7 31.5 %shard_map.76.hidden_ref.refs_0_ = bf16[256,2560]{1,0:T(8,128)(2,1)} custom-call(s32[4]{0:T(128)S(1)} %and_select_fusion.places_ref, bf16[64,2560]{1,0:T(8,128)(2,1)S(1)} %copy-done.11, bf16[64,2560]{1,0:T(8,128)(2,1)} %collective-permute-done.refs_1_, bf16[64,2560]{1,0:T(8,128)(2,1)} %collective-permute-done.1.refs_2_, ...), custom_call_target="tpu_custom_call" | custom-call | bytes 2621440 | tf_op jit(solution)/shard_map/pallas_call | solution.py:293
  79.4 2.1 %copy-done.1 = bf16[2560,768]{1,0:T(8,128)(2,1)S(1)} copy-done((bf16[2560,768]{1,0:T(8,128)(2,1)S(1)}, bf16[2560,768]{1,0:T(8,128)(2,1)}, u32[]{:S(2)}) %copy-start.1) | copy-done | bytes 3932184
  81.5 4.1 %shard_map.77 = (f32[256,768]{1,0:T(8,128)S(1)}, f32[8,256]{1,0:T(8,128)S(1)}) custom-call(s32[2]{0:T(128)S(1)} %pad_add_fusion.1.core_ref, bf16[256,2560]{1,0:T(8,128)(2,1)} %shard_map.76.hidden_ref.refs_0_, bf16[2560,768]{1,0:T(8,128)(2,1)S(1)} %copy-done.1, f32[2,256]{1,0:T(2,128)S(1)} %convert_bitcast_fusion.1.ids_ref), custom_call_target="tpu_custom_call" | custom-call | flops 1006632960 | bytes 4718592 | tf_op jit(solution)/shard_map/pallas_call | solution.py:145
  85.5 0.9 copy-done.4
  86.4 3.8 %shard_map.78 = (f32[256,768]{1,0:T(8,128)S(1)}, f32[8,256]{1,0:T(8,128)S(1)}) custom-call(s32[2]{0:T(128)S(1)} %pad_add_fusion.1.core_ref, bf16[256,2560]{1,0:T(8,128)(2,1)} %collective-permute-done.3.hidden_ref.refs_1_, bf16[2560,768]{1,0:T(8,128)(2,1)S(1)} %copy-done.2, f32[2,256]{1,0:T(2,128)S(1)} %convert_bitcast_fusion.1.ids_ref), custom_call_target="tpu_custom_call" | custom-call | flops 1006632960 | bytes 4718592 | tf_op jit(solution)/shard_map/pallas_call | solution.py:145
  90.3 0.9 copy-done.7
  91.1 2.1 %collective-permute-start.7 = (f32[4,512]{1,0:T(4,128)S(1)}, f32[4,512]{1,0:T(4,128)S(1)}, u32[]{:S(2)}, u32[]{:S(2)}) collective-permute-start(f32[4,512]{1,0:T(4,128)S(1)} %bitcast.90), channel_id=1, source_target_pairs={{0,6},{2,0},{4,2},{6,4},{1,7},{3,1},{5,3},{7,5},{8,14},{10,8},{12,... | collective-permute-start | bytes 24584 | tf_op jit(solution)/shard_map/ppermute | solution.py:351
  93.3 1.1 collective-permute-start.6
  94.9 2.3 %shard_map.81 = bf16[512,2560]{1,0:T(8,128)(2,1)S(1)} custom-call(s32[2]{0:T(128)S(1)} %iota.7.places_ref, bf16[256,2560]{1,0:T(8,128)(2,1)} %shard_map.76.hidden_ref.refs_0_, bf16[256,2560]{1,0:T(8,128)(2,1)} %collective-permute-done.3.hidden_ref.refs_1_), custom_call_target="tpu_custom_call" | custom-call | bytes 5242880 | tf_op jit(solution)/shard_map/pallas_call | solution.py:293
  97.1 1.5 copy-done.9
  100.9 1.1 copy-done.5
  102.0 1.1 copy-done.8
  103.1 3.3 %shard_map.79 = (f32[256,768]{1,0:T(8,128)S(1)}, f32[256,768]{1,0:T(8,128)S(1)}, f32[8,128]{1,0:T(8,128)S(1)}) custom-call(s32[2]{0:T(128)S(1)} %pad_add_fusion.1.core_ref, s32[8,264,384]{2,1,0:T(8,128)S(1)} %all-to-all-done.words_ref, f32[256,768]{1,0:T(8,128)S(1)} %copy-done.5, f32[256,768]{1,0:T(8,128)S(1)} %copy-done.8), custom_call_target="tpu_custom_call" | custom-call | flops 603979776 | bytes 7864320 | tf_op jit(solution)/shard_map/pallas_call | solution.py:145
  108.5 23.1 %all_to_all.20.shares_ref = f32[64,16,128]{2,1,0:T(8,128)S(1)} all-to-all(f32[64,16,128]{2,1,0:T(8,128)S(1)} %shard_map.80), channel_id=1, replica_groups=mesh['xh'=2,'xl'=2,'yh'=2,'yl'=2,'z'=4,'c'=2] {'z','yh','xh','yl','xl'}, dimensions={0} | all-to-all | bytes 1048576 | tf_op jit(solution)/shard_map/all_to_all | solution.py:361
  131.5 2.4 %shard_map.82 = (bf16[256,768]{1,0:T(8,128)(2,1)S(1)}, bf16[256,768]{1,0:T(8,128)(2,1)S(1)}, f32[8,256]{1,0:T(8,128)S(1)}) custom-call(s32[2]{0:T(128)S(1)} %pad_add_fusion.1.core_ref, f32[64,16,128]{2,1,0:T(8,128)S(1)} %all_to_all.20.shares_ref, f32[2,256]{1,0:T(2,128)S(1)} %convert_bitcast_fusion.1.ids_ref, f32[256,768]{1,0:T(8,128)S(1)} %copy-done.6, ...), custom_call_target="tpu_custom_call" | custom-call | flops 7864320 | bytes 4718592 | tf_op jit(solution)/shard_map/pallas_call | solution.py:145
  133.9 1.2 fusion.32
  135.8 4.2 %convolution_convert_fusion = bf16[2560,768]{1,0:T(8,128)(2,1)} fusion(bf16[512,2560]{1,0:T(8,128)(2,1)S(1)} %copy-done.10, bf16[256,768]{1,0:T(8,128)(2,1)S(1)} %get-tuple-element.39, bf16[256,768]{1,0:T(8,128)(2,1)S(1)} %get-tuple-element.38), kind=kOutput, calls=%fused_computation.4 | convolution fusion | flops 2016804864 | bytes 7340032 | tf_op jit(solution)/shard_map/dot_general | solution.py:371
  140.1 1.2 fusion.2
  141.7 26.9 %all_to_all.21 = bf16[64,4,2560]{2,1,0:T(4,128)(2,1)S(1)} all-to-all(bf16[64,4,2560]{2,1,0:T(4,128)(2,1)S(1)} %reshape.125), channel_id=1, replica_groups=mesh['xh'=2,'xl'=2,'yh'=2,'yl'=2,'z'=4,'c'=2] {'z','yh','yl','xh','xl'}, dimensions={0} | all-to-all | bytes 2621440 | tf_op jit(solution)/shard_map/all_to_all | solution.py:378
  (60 shorter events, 8.3 us)
Async XLA Ops:
  0.6 8.8 %copy-start = (bf16[256,512]{1,0:T(8,128)(2,1)S(1)}, bf16[256,512]{1,0:T(8,128)(2,1)}, u32[]{:S(2)}) copy-start(bf16[256,512]{1,0:T(8,128)(2,1)} %param.7) | copy-start | bytes 786436
  2.3 16.6 %all-to-all-start.1 = ((bf16[16,4,2560]{2,1,0:T(4,128)(2,1)}), bf16[16,4,2560]{2,1,0:T(4,128)(2,1)}, u32[]{:S(2)}, u32[]{:S(2)}) async-start(bf16[16,4,2560]{2,1,0:T(4,128)(2,1)} %broadcast_in_dim.2), calls=%async_computation.1 | async-start | bytes 655360 | tf_op jit(solution)/shard_map/all_to_all | solution.py:319
  18.9 80.5 %all-to-all-start = ((s32[8,264,384]{2,1,0:T(8,128)}), s32[8,264,384]{2,1,0:T(8,128)S(1)}, u32[]{:S(2)}, u32[]{:S(2)}) async-start(s32[8,264,384]{2,1,0:T(8,128)} %bitcast.87), calls=%async_computation | async-start | bytes 6488064 | tf_op jit(solution)/shard_map/all_to_all | solution.py:335
  25.5 53.9 %copy-start.12 = (s32[256,2]{0,1:T(2,128)S(1)}, s32[256,2]{0,1:T(2,128)}, u32[]{:S(2)}) copy-start(s32[256,2]{0,1:T(2,128)} %param.11) | copy-start | bytes 6148
  27.3 12.1 %collective-permute-start = (bf16[64,2560]{1,0:T(8,128)(2,1)}, bf16[64,2560]{1,0:T(8,128)(2,1)}, u32[]{:S(2)}, u32[]{:S(2)}) collective-permute-start(bf16[64,2560]{1,0:T(8,128)(2,1)} %reshape.123.refs_0_), channel_id=1, source_target_pairs={{0,2},{2,4},{4,6},{6,0},{1,3},{3,5},{5,7},{7,1},{8,10},{10,12},{12... | collective-permute-start | bytes 983048 | tf_op jit(solution)/shard_map/ppermute | solution.py:313
  29.2 17.5 %collective-permute-start.1 = (bf16[64,2560]{1,0:T(8,128)(2,1)}, bf16[64,2560]{1,0:T(8,128)(2,1)}, u32[]{:S(2)}, u32[]{:S(2)}) collective-permute-start(bf16[64,2560]{1,0:T(8,128)(2,1)} %reshape.123.refs_0_), channel_id=1, source_target_pairs={{0,4},{2,6},{4,0},{6,2},{1,5},{3,7},{5,1},{7,3},{8,12},{10,14},{12... | collective-permute-start | bytes 983048 | tf_op jit(solution)/shard_map/ppermute | solution.py:313
  32.8 13.9 %collective-permute-start.2 = (bf16[64,2560]{1,0:T(8,128)(2,1)}, bf16[64,2560]{1,0:T(8,128)(2,1)}, u32[]{:S(2)}, u32[]{:S(2)}) collective-permute-start(bf16[64,2560]{1,0:T(8,128)(2,1)} %reshape.123.refs_0_), channel_id=1, source_target_pairs={{0,6},{2,0},{4,2},{6,4},{1,7},{3,1},{5,3},{7,5},{8,14},{10,8},{12,... | collective-permute-start | bytes 983048 | tf_op jit(solution)/shard_map/ppermute | solution.py:313
  46.7 1.0 copy-start.11
  79.2 7.3 %collective-permute-start.3 = (bf16[256,2560]{1,0:T(8,128)(2,1)}, bf16[256,2560]{1,0:T(8,128)(2,1)}, u32[]{:S(2)}, u32[]{:S(2)}) collective-permute-start(bf16[256,2560]{1,0:T(8,128)(2,1)} %shard_map.76.hidden_ref.refs_0_), channel_id=1, source_target_pairs={{0,1},{1,0},{2,3},{3,2},{4,5},{5,4},{6,7},{7,6},{8,9},{9,8},{10,11... | collective-permute-start | bytes 3932168 | tf_op jit(solution)/shard_map/ppermute | solution.py:341
  79.4 2.1 %copy-start.1 = (bf16[2560,768]{1,0:T(8,128)(2,1)S(1)}, bf16[2560,768]{1,0:T(8,128)(2,1)}, u32[]{:S(2)}) copy-start(bf16[2560,768]{1,0:T(8,128)(2,1)} %head_ref.3) | copy-start | bytes 11796484
  81.5 5.0 %copy-start.2 = (bf16[2560,768]{1,0:T(8,128)(2,1)S(1)}, bf16[2560,768]{1,0:T(8,128)(2,1)}, u32[]{:S(2)}) copy-start(bf16[2560,768]{1,0:T(8,128)(2,1)} %head_ref.3) | copy-start | bytes 11796484
  85.5 0.9 copy-start.4
  90.2 0.9 copy-start.7
  91.1 7.5 %collective-permute-start.7 = (f32[4,512]{1,0:T(4,128)S(1)}, f32[4,512]{1,0:T(4,128)S(1)}, u32[]{:S(2)}, u32[]{:S(2)}) collective-permute-start(f32[4,512]{1,0:T(4,128)S(1)} %bitcast.90), channel_id=1, source_target_pairs={{0,6},{2,0},{4,2},{6,4},{1,7},{3,1},{5,3},{7,5},{8,14},{10,8},{12,... | collective-permute-start | bytes 24584 | tf_op jit(solution)/shard_map/ppermute | solution.py:351
  93.3 5.4 %collective-permute-start.6 = (f32[4,512]{1,0:T(4,128)S(1)}, f32[4,512]{1,0:T(4,128)S(1)}, u32[]{:S(2)}, u32[]{:S(2)}) collective-permute-start(f32[4,512]{1,0:T(4,128)S(1)} %bitcast.91), channel_id=1, source_target_pairs={{0,4},{2,6},{4,0},{6,2},{1,5},{3,7},{5,1},{7,3},{8,12},{10,14},{12... | collective-permute-start | bytes 24584 | tf_op jit(solution)/shard_map/ppermute | solution.py:351
  94.4 4.9 %collective-permute-start.5 = (f32[4,512]{1,0:T(4,128)S(1)}, f32[4,512]{1,0:T(4,128)S(1)}, u32[]{:S(2)}, u32[]{:S(2)}) collective-permute-start(f32[4,512]{1,0:T(4,128)S(1)} %bitcast.92), channel_id=1, source_target_pairs={{0,2},{2,4},{4,6},{6,0},{1,3},{3,5},{5,7},{7,1},{8,10},{10,12},{12... | collective-permute-start | bytes 24584 | tf_op jit(solution)/shard_map/ppermute | solution.py:351
  97.1 1.5 copy-start.9
  100.6 6.5 %collective-permute-start.8 = (f32[4,128]{1,0:T(4,128)S(1)}, f32[4,128]{1,0:T(4,128)S(1)}, u32[]{:S(2)}, u32[]{:S(2)}) collective-permute-start(f32[4,128]{1,0:T(4,128)S(1)} %bitcast.95), channel_id=1, source_target_pairs={{0,1},{1,0},{2,3},{3,2},{4,5},{5,4},{6,7},{7,6},{8,9},{9,8},{10,11... | collective-permute-start | bytes 6152 | tf_op jit(solution)/shard_map/ppermute | solution.py:355
  100.8 1.1 copy-start.5
  102.0 1.1 copy-start.8
  103.1 28.4 %copy-start.6 = (f32[256,768]{1,0:T(8,128)S(1)}, f32[256,768]{1,0:T(8,128)}, u32[]{:S(2)}) copy-start(f32[256,768]{1,0:T(8,128)} %copy-done.4) | copy-start | bytes 2359300
  106.5 27.4 %copy-start.3 = (bf16[2560,768]{1,0:T(8,128)(2,1)S(1)}, bf16[2560,768]{1,0:T(8,128)(2,1)}, u32[]{:S(2)}) copy-start(bf16[2560,768]{1,0:T(8,128)(2,1)} %head_ref.3) | copy-start | bytes 11796484
  106.5 1.4 collective-permute-start.4
  133.9 1.9 %copy-start.10 = (bf16[512,2560]{1,0:T(8,128)(2,1)S(1)}, bf16[512,2560]{1,0:T(8,128)(2,1)}, u32[]{:S(2)}) copy-start(bf16[512,2560]{1,0:T(8,128)(2,1)} %copy-done.9) | copy-start | bytes 7864324
  135.1 5.0 %collective-permute-start.9 = (f32[256,2560]{1,0:T(8,128)S(1)}, f32[256,2560]{1,0:T(8,128)S(1)}, u32[]{:S(2)}, u32[]{:S(2)}) collective-permute-start(f32[256,2560]{1,0:T(8,128)S(1)} %fusion.32), channel_id=1, source_target_pairs={{0,1},{1,0},{2,3},{3,2},{4,5},{5,4},{6,7},{7,6},{8,9},{9,8},{10,11... | collective-permute-start | bytes 7864328 | tf_op jit(solution)/shard_map/ppermute | solution.py:368

commit v3 on v2

--- a/solution.py
+++ b/solution.py
@@ -275,34 +275,19 @@
 
 
 def place_kernel(count, places_ref, *refs):
-    blocks, out_ref, sems = refs[:count], refs[count], refs[count + 1]
+    blocks, out_ref = refs[:count], refs[count]
     rows = blocks[0].shape[0]
-    copies = []
     for i, block in enumerate(blocks):
         at = pl.multiple_of(places_ref[i] * rows, rows)
-        copies.append(pltpu.make_async_copy(block, out_ref.at[pl.ds(at, rows), :], sems.at[i]))
-    for copy in copies:
-        copy.start()
-    for copy in copies:
-        copy.wait()
+        out_ref[pl.ds(at, rows), :] = block[...]
 
 
 def place_blocks(places, *blocks):
     count = len(blocks)
     rows, width = blocks[0].shape
-    return pl.pallas_call(
-        functools.partial(place_kernel, count),
-        out_shape=jax.ShapeDtypeStruct((count * rows, width), blocks[0].dtype),
-        grid_spec=pltpu.PrefetchScalarGridSpec(
-            num_scalar_prefetch=1,
-            grid=(1,),
-            in_specs=[pl.BlockSpec(memory_space=pl.ANY)] * count,
-            out_specs=pl.BlockSpec(memory_space=pl.ANY),
-            scratch_shapes=[pltpu.SemaphoreType.DMA((count,))],
-        ),
-        compiler_params=pltpu.CompilerParams(vmem_limit_bytes=2 << 20),
-        cost_estimate=pl.CostEstimate(flops=0, bytes_accessed=2 * count * blocks[0].size * 2, transcendentals=0),
-    )(places, *blocks)
+    result = jax.ShapeDtypeStruct((count * rows, width), blocks[0].dtype)
+    cost = (0, 4 * result.size, 0)
+    return call(functools.partial(place_kernel, count), places, blocks, (result,), GRANT, cost)[0]
 
 
 def ring_gather(block, axis):

time: 170 us -> 142 us (0.84)
  Pallas kernels: 47.9 us -> 19.4 us
    pallas_call x2 -> x0, Pallas kernels: 33.7 us -> none  [place_blocks(): pl.pallas_call(functools.partial(place_kernel, count), out_shape=jax.Shap...]
    pallas_call x5 -> x7, Pallas kernels: 14.2 us -> 19.4 us  [call(): pl.pallas_call(kernel, out_shape=tuple(results), grid_spec=pltpu.Prefetch...]
  transfers between devices with their start and end apart: 12 -> 12, of which waited for: 6 -> 6; matrix products, arithmetic and copies ran while one was open for 9% -> 11% of each run, Pallas kernels for 26% -> 12%
where the time goes in v3:
time: 142 us
  blocking collectives  50.4 us (35%)
  starting transfers between devices  24.9 us (18%)
  Pallas kernels  19.4 us (14%)
  local copies, waits for them, and re-layouts  16 us (11%)
  waiting for transfers between devices  14.7 us (10%)
  matrix products  12.3 us (9%)
  other arithmetic  2.15 us (2%)
  between operations  1.54 us (1%)
    all_to_all x1, blocking collectives, local(): share = lax.all_to_all(share, WALK, 0, 0, tiled=True)  26.9 us
    all_to_all x1, blocking collectives, local(): shares = lax.all_to_all(copies, EXCHANGE, 0, 0, tiled=True)  23.5 us
    pallas_call x7, Pallas kernels, call(): pl.pallas_call(kernel, out_shape=tuple(results), grid_spec=pltpu.Prefetch...  19.4 us
    ppermute x3, waiting for transfers between devices, ring_gather(): lax.ppermute(block, axis, [(i, (i + step) % size) for i in range(size)])  12.9 us
    unnamed x27, local copies, waits for them, and re-layouts  9.28 us
    all_to_all x1, starting transfers between devices, everywhere(): return lax.all_to_all(copies, axes, 0, 0, tiled=True)  7.16 us
    all_to_all x1, starting transfers between devices, local(): words = lax.all_to_all(words, STRIPES, 0, 0, tiled=True)  6.61 us
    ppermute x3, starting transfers between devices, ring_gather(): lax.ppermute(block, axis, [(i, (i + step) % size) for i in range(size)])  6.53 us
  transfers between devices with their start and end apart: 12, of which 6 were waited for; matrix products, arithmetic and copies ran while one was open for 11% of the time, Pallas kernels for 12%

profile of v3, /device:TPU:0, one launch (start us, length us, event | category | flops | bytes accessed | tf_op | source)
XLA Modules:
  0.0 141.6 jit_solution(10889628916541487742)
XLA Ops:
  1.5 0.8 broadcast_in_dim.2
  2.3 7.2 %all-to-all-start.1 = ((bf16[16,4,2560]{2,1,0:T(4,128)(2,1)}), bf16[16,4,2560]{2,1,0:T(4,128)(2,1)}, u32[]{:S(2)}, u32[]{:S(2)}) async-start(bf16[16,4,2560]{2,1,0:T(4,128)(2,1)} %broadcast_in_dim.2), calls=%async_computation.1 | async-start | bytes 655360 | tf_op jit(solution)/shard_map/all_to_all | solution.py:304
  9.4 5.7 %abs_reduce_fusion = (f32[8,256]{1,0:T(8,128)S(1)}, f32[8,768,256]{1,2,0:T(8,128)S(1)}) fusion(bf16[512,8,768]{2,1,0:T(8,128)(2,1)} %param.8, bf16[256,512]{1,0:T(8,128)(2,1)S(1)} %copy-done), kind=kOutput, calls=%fused_computation.3 | convolution fusion | flops 1613756416 | bytes 12853248 | tf_op jit(solution)/shard_map/rd,dsv->srv/dot_general | solution.py:317
  15.2 0.8 convert_bitcast_fusion
  16.5 1.9 %copy.30 = s32[2,2,2,264,384]{4,3,0,1,2:T(8,128)} copy(s32[2,2,2,264,384]{4,3,2,1,0:T(8,128)S(1)} %bitcast.88) | data formatting | bytes 6488064 | tf_op jit(solution)/shard_map/reshape | solution.py:319
  18.9 6.6 %all-to-all-start = ((s32[8,264,384]{2,1,0:T(8,128)}), s32[8,264,384]{2,1,0:T(8,128)S(1)}, u32[]{:S(2)}, u32[]{:S(2)}) async-start(s32[8,264,384]{2,1,0:T(8,128)} %bitcast.87), calls=%async_computation | async-start | bytes 6488064 | tf_op jit(solution)/shard_map/all_to_all | solution.py:320
  25.5 1.8 %reshape.123.refs_0_ = bf16[64,2560]{1,0:T(8,128)(2,1)} reshape(bf16[16,4,2560]{2,1,0:T(4,128)(2,1)} %all-to-all-done.1) | data formatting | bytes 655360 | tf_op jit(solution)/shard_map/reshape | solution.py:323
  27.3 1.9 %collective-permute-start = (bf16[64,2560]{1,0:T(8,128)(2,1)}, bf16[64,2560]{1,0:T(8,128)(2,1)}, u32[]{:S(2)}, u32[]{:S(2)}) collective-permute-start(bf16[64,2560]{1,0:T(8,128)(2,1)} %reshape.123.refs_0_), channel_id=1, source_target_pairs={{0,2},{2,4},{4,6},{6,0},{1,3},{3,5},{5,7},{7,1},{8,10},{10,12},{12... | collective-permute-start | bytes 983048 | tf_op jit(solution)/shard_map/ppermute | solution.py:298
  29.2 3.6 %collective-permute-start.1 = (bf16[64,2560]{1,0:T(8,128)(2,1)}, bf16[64,2560]{1,0:T(8,128)(2,1)}, u32[]{:S(2)}, u32[]{:S(2)}) collective-permute-start(bf16[64,2560]{1,0:T(8,128)(2,1)} %reshape.123.refs_0_), channel_id=1, source_target_pairs={{0,4},{2,6},{4,0},{6,2},{1,5},{3,7},{5,1},{7,3},{8,12},{10,14},{12... | collective-permute-start | bytes 983048 | tf_op jit(solution)/shard_map/ppermute | solution.py:298
  32.8 1.0 collective-permute-start.2
  33.8 5.5 %collective-permute-done.refs_1_ = bf16[64,2560]{1,0:T(8,128)(2,1)} collective-permute-done((bf16[64,2560]{1,0:T(8,128)(2,1)}, bf16[64,2560]{1,0:T(8,128)(2,1)}, u32[]{:S(2)}, u32[]{:S(2)}) %collective-permute-start) | collective-permute-done | bytes 327712 | tf_op jit(solution)/shard_map/ppermute | solution.py:298
  39.4 7.4 %collective-permute-done.1.refs_2_ = bf16[64,2560]{1,0:T(8,128)(2,1)} collective-permute-done((bf16[64,2560]{1,0:T(8,128)(2,1)}, bf16[64,2560]{1,0:T(8,128)(2,1)}, u32[]{:S(2)}, u32[]{:S(2)}) %collective-permute-start.1) | collective-permute-done | bytes 327712 | tf_op jit(solution)/shard_map/ppermute | solution.py:298
  46.7 1.0 copy-done.11
  47.7 2.9 %shard_map.76.hidden_ref.refs_0_ = bf16[256,2560]{1,0:T(8,128)(2,1)} custom-call(s32[4]{0:T(128)S(1)} %and_select_fusion.places_ref, bf16[64,2560]{1,0:T(8,128)(2,1)S(1)} %copy-done.11, bf16[64,2560]{1,0:T(8,128)(2,1)} %collective-permute-done.refs_1_, bf16[64,2560]{1,0:T(8,128)(2,1)} %collective-permute-done.1.refs_2_, ...), custom_call_target="tpu_custom_call" | custom-call | bytes 2621440 | tf_op jit(solution)/shard_map/pallas_call | solution.py:145
  50.6 2.1 %copy-done.1 = bf16[2560,768]{1,0:T(8,128)(2,1)S(1)} copy-done((bf16[2560,768]{1,0:T(8,128)(2,1)S(1)}, bf16[2560,768]{1,0:T(8,128)(2,1)}, u32[]{:S(2)}) %copy-start.1) | copy-done | bytes 3932184
  52.8 4.1 %shard_map.77 = (f32[256,768]{1,0:T(8,128)S(1)}, f32[8,256]{1,0:T(8,128)S(1)}) custom-call(s32[2]{0:T(128)S(1)} %pad_add_fusion.1.core_ref, bf16[256,2560]{1,0:T(8,128)(2,1)} %shard_map.76.hidden_ref.refs_0_, bf16[2560,768]{1,0:T(8,128)(2,1)S(1)} %copy-done.1, f32[2,256]{1,0:T(2,128)S(1)} %convert_bitcast_fusion.1.ids_ref), custom_call_target="tpu_custom_call" | custom-call | flops 1006632960 | bytes 4718592 | tf_op jit(solution)/shard_map/pallas_call | solution.py:145
  56.8 0.9 copy-done.4
  57.7 3.8 %shard_map.78 = (f32[256,768]{1,0:T(8,128)S(1)}, f32[8,256]{1,0:T(8,128)S(1)}) custom-call(s32[2]{0:T(128)S(1)} %pad_add_fusion.1.core_ref, bf16[256,2560]{1,0:T(8,128)(2,1)} %collective-permute-done.3.hidden_ref.refs_1_, bf16[2560,768]{1,0:T(8,128)(2,1)S(1)} %copy-done.2, f32[2,256]{1,0:T(2,128)S(1)} %convert_bitcast_fusion.1.ids_ref), custom_call_target="tpu_custom_call" | custom-call | flops 1006632960 | bytes 4718592 | tf_op jit(solution)/shard_map/pallas_call | solution.py:145
  61.5 0.9 copy-done.7
  62.4 2.1 %collective-permute-start.7 = (f32[4,512]{1,0:T(4,128)S(1)}, f32[4,512]{1,0:T(4,128)S(1)}, u32[]{:S(2)}, u32[]{:S(2)}) collective-permute-start(f32[4,512]{1,0:T(4,128)S(1)} %bitcast.90), channel_id=1, source_target_pairs={{0,6},{2,0},{4,2},{6,4},{1,7},{3,1},{5,3},{7,5},{8,14},{10,8},{12,... | collective-permute-start | bytes 24584 | tf_op jit(solution)/shard_map/ppermute | solution.py:336
  64.6 1.1 collective-permute-start.6
  66.1 2.4 %shard_map.81 = bf16[512,2560]{1,0:T(8,128)(2,1)S(1)} custom-call(s32[2]{0:T(128)S(1)} %iota.7.places_ref, bf16[256,2560]{1,0:T(8,128)(2,1)} %shard_map.76.hidden_ref.refs_0_, bf16[256,2560]{1,0:T(8,128)(2,1)} %collective-permute-done.3.hidden_ref.refs_1_), custom_call_target="tpu_custom_call" | custom-call | bytes 5242880 | tf_op jit(solution)/shard_map/pallas_call | solution.py:145
  68.6 1.5 %copy-done.9 = bf16[512,2560]{1,0:T(8,128)(2,1)} copy-done((bf16[512,2560]{1,0:T(8,128)(2,1)}, bf16[512,2560]{1,0:T(8,128)(2,1)S(1)}, u32[]{:S(2)}) %copy-start.9) | copy-done | bytes 2621464
  72.1 1.1 copy-done.5
  73.3 1.1 copy-done.8
  74.4 3.3 %shard_map.79 = (f32[256,768]{1,0:T(8,128)S(1)}, f32[256,768]{1,0:T(8,128)S(1)}, f32[8,128]{1,0:T(8,128)S(1)}) custom-call(s32[2]{0:T(128)S(1)} %pad_add_fusion.1.core_ref, s32[8,264,384]{2,1,0:T(8,128)S(1)} %all-to-all-done.words_ref, f32[256,768]{1,0:T(8,128)S(1)} %copy-done.5, f32[256,768]{1,0:T(8,128)S(1)} %copy-done.8), custom_call_target="tpu_custom_call" | custom-call | flops 603979776 | bytes 7864320 | tf_op jit(solution)/shard_map/pallas_call | solution.py:145
  79.8 23.5 %all_to_all.20.shares_ref = f32[64,16,128]{2,1,0:T(8,128)S(1)} all-to-all(f32[64,16,128]{2,1,0:T(8,128)S(1)} %shard_map.80), channel_id=1, replica_groups=mesh['xh'=2,'xl'=2,'yh'=2,'yl'=2,'z'=4,'c'=2] {'z','yh','xh','yl','xl'}, dimensions={0} | all-to-all | bytes 1048576 | tf_op jit(solution)/shard_map/all_to_all | solution.py:346
  103.3 2.4 %shard_map.82 = (bf16[256,768]{1,0:T(8,128)(2,1)S(1)}, bf16[256,768]{1,0:T(8,128)(2,1)S(1)}, f32[8,256]{1,0:T(8,128)S(1)}) custom-call(s32[2]{0:T(128)S(1)} %pad_add_fusion.1.core_ref, f32[64,16,128]{2,1,0:T(8,128)S(1)} %all_to_all.20.shares_ref, f32[2,256]{1,0:T(2,128)S(1)} %convert_bitcast_fusion.1.ids_ref, f32[256,768]{1,0:T(8,128)S(1)} %copy-done.6, ...), custom_call_target="tpu_custom_call" | custom-call | flops 7864320 | bytes 4718592 | tf_op jit(solution)/shard_map/pallas_call | solution.py:145
  105.7 1.2 fusion.32
  107.6 4.2 %convolution_convert_fusion = bf16[2560,768]{1,0:T(8,128)(2,1)} fusion(bf16[512,2560]{1,0:T(8,128)(2,1)S(1)} %copy-done.10, bf16[256,768]{1,0:T(8,128)(2,1)S(1)} %get-tuple-element.39, bf16[256,768]{1,0:T(8,128)(2,1)S(1)} %get-tuple-element.38), kind=kOutput, calls=%fused_computation.4 | convolution fusion | flops 2016804864 | bytes 7340032 | tf_op jit(solution)/shard_map/dot_general | solution.py:356
  111.9 1.2 fusion.2
  113.5 26.9 %all_to_all.21 = bf16[64,4,2560]{2,1,0:T(4,128)(2,1)S(1)} all-to-all(bf16[64,4,2560]{2,1,0:T(4,128)(2,1)S(1)} %reshape.125), channel_id=1, replica_groups=mesh['xh'=2,'xl'=2,'yh'=2,'yl'=2,'z'=4,'c'=2] {'z','yh','yl','xh','xl'}, dimensions={0} | all-to-all | bytes 2621440 | tf_op jit(solution)/shard_map/all_to_all | solution.py:363
  (60 shorter events, 8.0 us)
Async XLA Ops:
  0.6 8.8 %copy-start = (bf16[256,512]{1,0:T(8,128)(2,1)S(1)}, bf16[256,512]{1,0:T(8,128)(2,1)}, u32[]{:S(2)}) copy-start(bf16[256,512]{1,0:T(8,128)(2,1)} %param.7) | copy-start | bytes 786436
  2.3 16.6 %all-to-all-start.1 = ((bf16[16,4,2560]{2,1,0:T(4,128)(2,1)}), bf16[16,4,2560]{2,1,0:T(4,128)(2,1)}, u32[]{:S(2)}, u32[]{:S(2)}) async-start(bf16[16,4,2560]{2,1,0:T(4,128)(2,1)} %broadcast_in_dim.2), calls=%async_computation.1 | async-start | bytes 655360 | tf_op jit(solution)/shard_map/all_to_all | solution.py:304
  18.9 51.8 %all-to-all-start = ((s32[8,264,384]{2,1,0:T(8,128)}), s32[8,264,384]{2,1,0:T(8,128)S(1)}, u32[]{:S(2)}, u32[]{:S(2)}) async-start(s32[8,264,384]{2,1,0:T(8,128)} %bitcast.87), calls=%async_computation | async-start | bytes 6488064 | tf_op jit(solution)/shard_map/all_to_all | solution.py:320
  25.5 25.1 %copy-start.12 = (s32[256,2]{0,1:T(2,128)S(1)}, s32[256,2]{0,1:T(2,128)}, u32[]{:S(2)}) copy-start(s32[256,2]{0,1:T(2,128)} %param.11) | copy-start | bytes 6148
  27.3 12.1 %collective-permute-start = (bf16[64,2560]{1,0:T(8,128)(2,1)}, bf16[64,2560]{1,0:T(8,128)(2,1)}, u32[]{:S(2)}, u32[]{:S(2)}) collective-permute-start(bf16[64,2560]{1,0:T(8,128)(2,1)} %reshape.123.refs_0_), channel_id=1, source_target_pairs={{0,2},{2,4},{4,6},{6,0},{1,3},{3,5},{5,7},{7,1},{8,10},{10,12},{12... | collective-permute-start | bytes 983048 | tf_op jit(solution)/shard_map/ppermute | solution.py:298
  29.2 17.5 %collective-permute-start.1 = (bf16[64,2560]{1,0:T(8,128)(2,1)}, bf16[64,2560]{1,0:T(8,128)(2,1)}, u32[]{:S(2)}, u32[]{:S(2)}) collective-permute-start(bf16[64,2560]{1,0:T(8,128)(2,1)} %reshape.123.refs_0_), channel_id=1, source_target_pairs={{0,4},{2,6},{4,0},{6,2},{1,5},{3,7},{5,1},{7,3},{8,12},{10,14},{12... | collective-permute-start | bytes 983048 | tf_op jit(solution)/shard_map/ppermute | solution.py:298
  32.8 13.9 %collective-permute-start.2 = (bf16[64,2560]{1,0:T(8,128)(2,1)}, bf16[64,2560]{1,0:T(8,128)(2,1)}, u32[]{:S(2)}, u32[]{:S(2)}) collective-permute-start(bf16[64,2560]{1,0:T(8,128)(2,1)} %reshape.123.refs_0_), channel_id=1, source_target_pairs={{0,6},{2,0},{4,2},{6,4},{1,7},{3,1},{5,3},{7,5},{8,14},{10,8},{12,... | collective-permute-start | bytes 983048 | tf_op jit(solution)/shard_map/ppermute | solution.py:298
  46.7 1.0 copy-start.11
  50.6 7.2 %collective-permute-start.3 = (bf16[256,2560]{1,0:T(8,128)(2,1)}, bf16[256,2560]{1,0:T(8,128)(2,1)}, u32[]{:S(2)}, u32[]{:S(2)}) collective-permute-start(bf16[256,2560]{1,0:T(8,128)(2,1)} %shard_map.76.hidden_ref.refs_0_), channel_id=1, source_target_pairs={{0,1},{1,0},{2,3},{3,2},{4,5},{5,4},{6,7},{7,6},{8,9},{9,8},{10,11... | collective-permute-start | bytes 3932168 | tf_op jit(solution)/shard_map/ppermute | solution.py:326
  50.6 2.1 %copy-start.1 = (bf16[2560,768]{1,0:T(8,128)(2,1)S(1)}, bf16[2560,768]{1,0:T(8,128)(2,1)}, u32[]{:S(2)}) copy-start(bf16[2560,768]{1,0:T(8,128)(2,1)} %head_ref.3) | copy-start | bytes 11796484
  52.8 5.0 %copy-start.2 = (bf16[2560,768]{1,0:T(8,128)(2,1)S(1)}, bf16[2560,768]{1,0:T(8,128)(2,1)}, u32[]{:S(2)}) copy-start(bf16[2560,768]{1,0:T(8,128)(2,1)} %head_ref.3) | copy-start | bytes 11796484
  56.8 0.9 copy-start.4
  61.5 0.9 copy-start.7
  62.4 7.7 %collective-permute-start.7 = (f32[4,512]{1,0:T(4,128)S(1)}, f32[4,512]{1,0:T(4,128)S(1)}, u32[]{:S(2)}, u32[]{:S(2)}) collective-permute-start(f32[4,512]{1,0:T(4,128)S(1)} %bitcast.90), channel_id=1, source_target_pairs={{0,6},{2,0},{4,2},{6,4},{1,7},{3,1},{5,3},{7,5},{8,14},{10,8},{12,... | collective-permute-start | bytes 24584 | tf_op jit(solution)/shard_map/ppermute | solution.py:336
  64.6 5.5 %collective-permute-start.6 = (f32[4,512]{1,0:T(4,128)S(1)}, f32[4,512]{1,0:T(4,128)S(1)}, u32[]{:S(2)}, u32[]{:S(2)}) collective-permute-start(f32[4,512]{1,0:T(4,128)S(1)} %bitcast.91), channel_id=1, source_target_pairs={{0,4},{2,6},{4,0},{6,2},{1,5},{3,7},{5,1},{7,3},{8,12},{10,14},{12... | collective-permute-start | bytes 24584 | tf_op jit(solution)/shard_map/ppermute | solution.py:336
  65.7 4.9 %collective-permute-start.5 = (f32[4,512]{1,0:T(4,128)S(1)}, f32[4,512]{1,0:T(4,128)S(1)}, u32[]{:S(2)}, u32[]{:S(2)}) collective-permute-start(f32[4,512]{1,0:T(4,128)S(1)} %bitcast.92), channel_id=1, source_target_pairs={{0,2},{2,4},{4,6},{6,0},{1,3},{3,5},{5,7},{7,1},{8,10},{10,12},{12... | collective-permute-start | bytes 24584 | tf_op jit(solution)/shard_map/ppermute | solution.py:336
  68.6 1.5 %copy-start.9 = (bf16[512,2560]{1,0:T(8,128)(2,1)}, bf16[512,2560]{1,0:T(8,128)(2,1)S(1)}, u32[]{:S(2)}) copy-start(bf16[512,2560]{1,0:T(8,128)(2,1)S(1)} %shard_map.81) | copy-start | bytes 7864324
  71.9 6.5 %collective-permute-start.8 = (f32[4,128]{1,0:T(4,128)S(1)}, f32[4,128]{1,0:T(4,128)S(1)}, u32[]{:S(2)}, u32[]{:S(2)}) collective-permute-start(f32[4,128]{1,0:T(4,128)S(1)} %bitcast.95), channel_id=1, source_target_pairs={{0,1},{1,0},{2,3},{3,2},{4,5},{5,4},{6,7},{7,6},{8,9},{9,8},{10,11... | collective-permute-start | bytes 6152 | tf_op jit(solution)/shard_map/ppermute | solution.py:340
  72.1 1.1 copy-start.5
  73.3 1.1 copy-start.8
  74.4 28.9 %copy-start.6 = (f32[256,768]{1,0:T(8,128)S(1)}, f32[256,768]{1,0:T(8,128)}, u32[]{:S(2)}) copy-start(f32[256,768]{1,0:T(8,128)} %copy-done.4) | copy-start | bytes 2359300
  77.8 27.9 %copy-start.3 = (bf16[2560,768]{1,0:T(8,128)(2,1)S(1)}, bf16[2560,768]{1,0:T(8,128)(2,1)}, u32[]{:S(2)}) copy-start(bf16[2560,768]{1,0:T(8,128)(2,1)} %head_ref.3) | copy-start | bytes 11796484
  77.8 1.4 collective-permute-start.4
  105.7 1.9 %copy-start.10 = (bf16[512,2560]{1,0:T(8,128)(2,1)S(1)}, bf16[512,2560]{1,0:T(8,128)(2,1)}, u32[]{:S(2)}) copy-start(bf16[512,2560]{1,0:T(8,128)(2,1)} %copy-done.9) | copy-start | bytes 7864324
  106.9 5.0 %collective-permute-start.9 = (f32[256,2560]{1,0:T(8,128)S(1)}, f32[256,2560]{1,0:T(8,128)S(1)}, u32[]{:S(2)}, u32[]{:S(2)}) collective-permute-start(f32[256,2560]{1,0:T(8,128)S(1)} %fusion.32), channel_id=1, source_target_pairs={{0,1},{1,0},{2,3},{3,2},{4,5},{5,4},{6,7},{7,6},{8,9},{9,8},{10,11... | collective-permute-start | bytes 7864328 | tf_op jit(solution)/shard_map/ppermute | solution.py:353

commit v4 on v3

--- a/solution.py
+++ b/solution.py
@@ -341,8 +341,6 @@
 
     own_teacher, other_teacher, tile = teacher_sum(scalars, words, own_scores, other_scores)
     copies = chip_copies(scalars, tile, lax.ppermute(tile, "c", pair), stats, chips)
-    hidden = place_blocks(jnp.arange(2, dtype=jnp.int32), own, other)
-    copies, hidden = lax.optimization_barrier((copies, hidden))
     shares = lax.all_to_all(copies, EXCHANGE, 0, 0, tiled=True)
     own_grad, other_grad, objective = slopes(
         scalars, shares, ids, own_scores, other_scores, own_teacher, other_teacher
@@ -353,6 +351,8 @@
     taken = lax.ppermute(give, "c", pair)
     keep = lax.dot_general(own_grad, student_head, contract, preferred_element_type=jnp.float32)
     grad = jnp.concatenate([own_grad, other_grad], axis=0)
+    late = (jnp.abs(own_grad[0, 0].astype(jnp.float32)) > 3e38).astype(jnp.int32)
+    hidden = place_blocks(jnp.arange(2, dtype=jnp.int32) + late, own, other)
     grad_head = lax.dot_general(
         hidden, grad, (((0,), (0,)), ((), ())), preferred_element_type=jnp.float32
     ).astype(jnp.bfloat16)

time: 142 us -> 146 us (1.028)
  waiting for transfers between devices: 14.7 us -> 18.6 us
    ppermute x3, waiting for transfers between devices: 0.48 us -> 4.43 us  [local(): lax.ppermute(stats, 'z', [(i, (i + j) % 4) for i in range(4)])]
    unnamed x27 -> x23, local copies, waits for them, and re-layouts: 9.28 us -> 7.78 us
  transfers between devices with their start and end apart: 12 -> 12, of which waited for: 6 -> 6; matrix products, arithmetic and copies ran while one was open for 11% -> 11% of each run, Pallas kernels for 12% -> 11%
where the time goes in v4:
time: 146 us; the launch traced here: 145 us
  blocking collectives  50.6 us (35%)
  starting transfers between devices  24.9 us (17%)
  Pallas kernels  19.5 us (13%)
  waiting for transfers between devices  18.6 us (13%)
  local copies, waits for them, and re-layouts  15.1 us (10%)
  matrix products  12.3 us (8%)
  between operations  2.19 us (2%)
  other arithmetic  2.15 us (1%)
    all_to_all x1, blocking collectives, local(): share = lax.all_to_all(share, WALK, 0, 0, tiled=True)  27.1 us
    all_to_all x1, blocking collectives, local(): shares = lax.all_to_all(copies, EXCHANGE, 0, 0, tiled=True)  23.5 us
    pallas_call x7, Pallas kernels, call(): pl.pallas_call(kernel, out_shape=tuple(results), grid_spec=pltpu.Prefetch...  19.5 us
    ppermute x3, waiting for transfers between devices, ring_gather(): lax.ppermute(block, axis, [(i, (i + step) % size) for i in range(size)])  12.9 us
    unnamed x23, local copies, waits for them, and re-layouts  7.78 us
    all_to_all x1, starting transfers between devices, everywhere(): return lax.all_to_all(copies, axes, 0, 0, tiled=True)  7.16 us
    all_to_all x1, starting transfers between devices, local(): words = lax.all_to_all(words, STRIPES, 0, 0, tiled=True)  6.61 us
    ppermute x3, starting transfers between devices, ring_gather(): lax.ppermute(block, axis, [(i, (i + step) % size) for i in range(size)])  6.53 us
  transfers between devices with their start and end apart: 12, of which 6 were waited for; matrix products, arithmetic and copies ran while one was open for 11% of the time, Pallas kernels for 11%

profile of v4, /device:TPU:0, one launch (start us, length us, event | category | flops | bytes accessed | tf_op | source)
XLA Modules:
  0.0 145.3 jit_solution(211803155444365476)
XLA Ops:
  1.5 0.8 broadcast_in_dim.2
  2.3 7.2 %all-to-all-start.1 = ((bf16[16,4,2560]{2,1,0:T(4,128)(2,1)}), bf16[16,4,2560]{2,1,0:T(4,128)(2,1)}, u32[]{:S(2)}, u32[]{:S(2)}) async-start(bf16[16,4,2560]{2,1,0:T(4,128)(2,1)} %broadcast_in_dim.2), calls=%async_computation.1 | async-start | bytes 655360 | tf_op jit(solution)/shard_map/all_to_all | solution.py:304
  9.5 5.7 %abs_reduce_fusion = (f32[8,256]{1,0:T(8,128)S(1)}, f32[8,768,256]{1,2,0:T(8,128)S(1)}) fusion(bf16[512,8,768]{2,1,0:T(8,128)(2,1)} %param.8, bf16[256,512]{1,0:T(8,128)(2,1)S(1)} %copy-done), kind=kOutput, calls=%fused_computation.3 | convolution fusion | flops 1613756416 | bytes 12853248 | tf_op jit(solution)/shard_map/rd,dsv->srv/dot_general | solution.py:317
  16.5 1.9 %copy.30 = s32[2,2,2,264,384]{4,3,0,1,2:T(8,128)} copy(s32[2,2,2,264,384]{4,3,2,1,0:T(8,128)S(1)} %bitcast.89) | data formatting | bytes 6488064 | tf_op jit(solution)/shard_map/reshape | solution.py:319
  18.9 6.6 %all-to-all-start = ((s32[8,264,384]{2,1,0:T(8,128)}), s32[8,264,384]{2,1,0:T(8,128)S(1)}, u32[]{:S(2)}, u32[]{:S(2)}) async-start(s32[8,264,384]{2,1,0:T(8,128)} %bitcast.88), calls=%async_computation | async-start | bytes 6488064 | tf_op jit(solution)/shard_map/all_to_all | solution.py:320
  25.5 1.8 %reshape.129.refs_0_ = bf16[64,2560]{1,0:T(8,128)(2,1)} reshape(bf16[16,4,2560]{2,1,0:T(4,128)(2,1)} %all-to-all-done.1) | data formatting | bytes 655360 | tf_op jit(solution)/shard_map/reshape | solution.py:323
  27.3 1.9 %collective-permute-start = (bf16[64,2560]{1,0:T(8,128)(2,1)}, bf16[64,2560]{1,0:T(8,128)(2,1)}, u32[]{:S(2)}, u32[]{:S(2)}) collective-permute-start(bf16[64,2560]{1,0:T(8,128)(2,1)} %reshape.129.refs_0_), channel_id=1, source_target_pairs={{0,2},{2,4},{4,6},{6,0},{1,3},{3,5},{5,7},{7,1},{8,10},{10,12},{12... | collective-permute-start | bytes 983048 | tf_op jit(solution)/shard_map/ppermute | solution.py:298
  29.2 3.6 %collective-permute-start.1 = (bf16[64,2560]{1,0:T(8,128)(2,1)}, bf16[64,2560]{1,0:T(8,128)(2,1)}, u32[]{:S(2)}, u32[]{:S(2)}) collective-permute-start(bf16[64,2560]{1,0:T(8,128)(2,1)} %reshape.129.refs_0_), channel_id=1, source_target_pairs={{0,4},{2,6},{4,0},{6,2},{1,5},{3,7},{5,1},{7,3},{8,12},{10,14},{12... | collective-permute-start | bytes 983048 | tf_op jit(solution)/shard_map/ppermute | solution.py:298
  32.8 1.0 collective-permute-start.2
  33.9 5.5 %collective-permute-done.refs_1_ = bf16[64,2560]{1,0:T(8,128)(2,1)} collective-permute-done((bf16[64,2560]{1,0:T(8,128)(2,1)}, bf16[64,2560]{1,0:T(8,128)(2,1)}, u32[]{:S(2)}, u32[]{:S(2)}) %collective-permute-start) | collective-permute-done | bytes 327712 | tf_op jit(solution)/shard_map/ppermute | solution.py:298
  39.4 7.4 %collective-permute-done.1.refs_2_ = bf16[64,2560]{1,0:T(8,128)(2,1)} collective-permute-done((bf16[64,2560]{1,0:T(8,128)(2,1)}, bf16[64,2560]{1,0:T(8,128)(2,1)}, u32[]{:S(2)}, u32[]{:S(2)}) %collective-permute-start.1) | collective-permute-done | bytes 327712 | tf_op jit(solution)/shard_map/ppermute | solution.py:298
  46.8 1.0 copy-done.9
  47.7 2.9 %shard_map.76.hidden_ref.refs_0_ = bf16[256,2560]{1,0:T(8,128)(2,1)} custom-call(s32[4]{0:T(128)S(1)} %and_select_fusion.places_ref, bf16[64,2560]{1,0:T(8,128)(2,1)S(1)} %copy-done.9, bf16[64,2560]{1,0:T(8,128)(2,1)} %collective-permute-done.refs_1_, bf16[64,2560]{1,0:T(8,128)(2,1)} %collective-permute-done.1.refs_2_, ...), custom_call_target="tpu_custom_call" | custom-call | bytes 2621440 | tf_op jit(solution)/shard_map/pallas_call | solution.py:145
  50.7 2.1 %copy-done.1 = bf16[2560,768]{1,0:T(8,128)(2,1)S(1)} copy-done((bf16[2560,768]{1,0:T(8,128)(2,1)S(1)}, bf16[2560,768]{1,0:T(8,128)(2,1)}, u32[]{:S(2)}) %copy-start.1) | copy-done | bytes 3932184
  52.8 4.1 %shard_map.77 = (f32[256,768]{1,0:T(8,128)S(1)}, f32[8,256]{1,0:T(8,128)S(1)}) custom-call(s32[2]{0:T(128)S(1)} %pad_add_fusion.1.core_ref, bf16[256,2560]{1,0:T(8,128)(2,1)} %shard_map.76.hidden_ref.refs_0_, bf16[2560,768]{1,0:T(8,128)(2,1)S(1)} %copy-done.1, f32[2,256]{1,0:T(2,128)S(1)} %convert_bitcast_fusion.1.ids_ref), custom_call_target="tpu_custom_call" | custom-call | flops 1006632960 | bytes 4718592 | tf_op jit(solution)/shard_map/pallas_call | solution.py:145
  56.9 0.9 copy-done.4
  57.8 3.8 %shard_map.78 = (f32[256,768]{1,0:T(8,128)S(1)}, f32[8,256]{1,0:T(8,128)S(1)}) custom-call(s32[2]{0:T(128)S(1)} %pad_add_fusion.1.core_ref, bf16[256,2560]{1,0:T(8,128)(2,1)} %collective-permute-done.3.hidden_ref.refs_1_, bf16[2560,768]{1,0:T(8,128)(2,1)S(1)} %copy-done.2, f32[2,256]{1,0:T(2,128)S(1)} %convert_bitcast_fusion.1.ids_ref), custom_call_target="tpu_custom_call" | custom-call | flops 1006632960 | bytes 4718592 | tf_op jit(solution)/shard_map/pallas_call | solution.py:145
  61.6 0.9 copy-done.7
  62.5 2.1 %collective-permute-start.7 = (f32[4,512]{1,0:T(4,128)S(1)}, f32[4,512]{1,0:T(4,128)S(1)}, u32[]{:S(2)}, u32[]{:S(2)}) collective-permute-start(f32[4,512]{1,0:T(4,128)S(1)} %bitcast.91), channel_id=1, source_target_pairs={{0,6},{2,0},{4,2},{6,4},{1,7},{3,1},{5,3},{7,5},{8,14},{10,8},{12,... | collective-permute-start | bytes 24584 | tf_op jit(solution)/shard_map/ppermute | solution.py:336
  64.6 1.1 collective-permute-start.6
  66.2 3.6 %collective-permute-done.6 = f32[4,512]{1,0:T(4,128)S(1)} collective-permute-done((f32[4,512]{1,0:T(4,128)S(1)}, f32[4,512]{1,0:T(4,128)S(1)}, u32[]{:S(2)}, u32[]{:S(2)}) %collective-permute-start.6) | collective-permute-done | bytes 8224 | tf_op jit(solution)/shard_map/ppermute | solution.py:336
  69.8 0.8 collective-permute-done.5
  72.2 1.1 copy-done.5
  73.3 1.1 copy-done.8
  74.5 3.3 %shard_map.79 = (f32[256,768]{1,0:T(8,128)S(1)}, f32[256,768]{1,0:T(8,128)S(1)}, f32[8,128]{1,0:T(8,128)S(1)}) custom-call(s32[2]{0:T(128)S(1)} %pad_add_fusion.1.core_ref, s32[8,264,384]{2,1,0:T(8,128)S(1)} %all-to-all-done.words_ref, f32[256,768]{1,0:T(8,128)S(1)} %copy-done.5, f32[256,768]{1,0:T(8,128)S(1)} %copy-done.8), custom_call_target="tpu_custom_call" | custom-call | flops 603979776 | bytes 7864320 | tf_op jit(solution)/shard_map/pallas_call | solution.py:145
  79.8 23.5 %all_to_all.20.shares_ref = f32[64,16,128]{2,1,0:T(8,128)S(1)} all-to-all(f32[64,16,128]{2,1,0:T(8,128)S(1)} %shard_map.80), channel_id=1, replica_groups=mesh['xh'=2,'xl'=2,'yh'=2,'yl'=2,'z'=4,'c'=2] {'z','yh','xh','yl','xl'}, dimensions={0} | all-to-all | bytes 1048576 | tf_op jit(solution)/shard_map/all_to_all | solution.py:344
  103.4 2.4 %shard_map.81 = (bf16[256,768]{1,0:T(8,128)(2,1)S(1)}, bf16[256,768]{1,0:T(8,128)(2,1)S(1)}, f32[8,256]{1,0:T(8,128)S(1)}) custom-call(s32[2]{0:T(128)S(1)} %pad_add_fusion.1.core_ref, f32[64,16,128]{2,1,0:T(8,128)S(1)} %all_to_all.20.shares_ref, f32[2,256]{1,0:T(2,128)S(1)} %convert_bitcast_fusion.1.ids_ref, f32[256,768]{1,0:T(8,128)S(1)} %copy-done.6, ...), custom_call_target="tpu_custom_call" | custom-call | flops 7864320 | bytes 4718592 | tf_op jit(solution)/shard_map/pallas_call | solution.py:145
  105.8 1.2 fusion.32
  108.3 2.4 %shard_map.82 = bf16[512,2560]{1,0:T(8,128)(2,1)S(1)} custom-call(s32[2]{0:T(128)S(1)} %iota_add_fusion.places_ref, bf16[256,2560]{1,0:T(8,128)(2,1)} %shard_map.76.hidden_ref.refs_0_, bf16[256,2560]{1,0:T(8,128)(2,1)} %collective-permute-done.3.hidden_ref.refs_1_), custom_call_target="tpu_custom_call" | custom-call | bytes 5242880 | tf_op jit(solution)/shard_map/pallas_call | solution.py:145
  111.3 4.2 %convolution_convert_fusion = bf16[2560,768]{1,0:T(8,128)(2,1)} fusion(bf16[512,2560]{1,0:T(8,128)(2,1)S(1)} %shard_map.82, bf16[256,768]{1,0:T(8,128)(2,1)S(1)} %get-tuple-element.36, bf16[256,768]{1,0:T(8,128)(2,1)S(1)} %get-tuple-element.35), kind=kOutput, calls=%fused_computation.4 | convolution fusion | flops 2016804864 | bytes 7340032 | tf_op jit(solution)/shard_map/dot_general | solution.py:356
  115.4 1.2 fusion.2
  117.0 27.1 %all_to_all.21 = bf16[64,4,2560]{2,1,0:T(4,128)(2,1)S(1)} all-to-all(bf16[64,4,2560]{2,1,0:T(4,128)(2,1)S(1)} %reshape.131), channel_id=1, replica_groups=mesh['xh'=2,'xl'=2,'yh'=2,'yl'=2,'z'=4,'c'=2] {'z','yh','yl','xh','xl'}, dimensions={0} | all-to-all | bytes 2621440 | tf_op jit(solution)/shard_map/all_to_all | solution.py:363
  (57 shorter events, 8.7 us)
Async XLA Ops:
  0.6 8.8 %copy-start = (bf16[256,512]{1,0:T(8,128)(2,1)S(1)}, bf16[256,512]{1,0:T(8,128)(2,1)}, u32[]{:S(2)}) copy-start(bf16[256,512]{1,0:T(8,128)(2,1)} %param.7) | copy-start | bytes 786436
  2.3 16.6 %all-to-all-start.1 = ((bf16[16,4,2560]{2,1,0:T(4,128)(2,1)}), bf16[16,4,2560]{2,1,0:T(4,128)(2,1)}, u32[]{:S(2)}, u32[]{:S(2)}) async-start(bf16[16,4,2560]{2,1,0:T(4,128)(2,1)} %broadcast_in_dim.2), calls=%async_computation.1 | async-start | bytes 655360 | tf_op jit(solution)/shard_map/all_to_all | solution.py:304
  18.9 51.8 %all-to-all-start = ((s32[8,264,384]{2,1,0:T(8,128)}), s32[8,264,384]{2,1,0:T(8,128)S(1)}, u32[]{:S(2)}, u32[]{:S(2)}) async-start(s32[8,264,384]{2,1,0:T(8,128)} %bitcast.88), calls=%async_computation | async-start | bytes 6488064 | tf_op jit(solution)/shard_map/all_to_all | solution.py:320
  25.5 25.2 %copy-start.10 = (s32[256,2]{0,1:T(2,128)S(1)}, s32[256,2]{0,1:T(2,128)}, u32[]{:S(2)}) copy-start(s32[256,2]{0,1:T(2,128)} %param.11) | copy-start | bytes 6148
  27.3 12.1 %collective-permute-start = (bf16[64,2560]{1,0:T(8,128)(2,1)}, bf16[64,2560]{1,0:T(8,128)(2,1)}, u32[]{:S(2)}, u32[]{:S(2)}) collective-permute-start(bf16[64,2560]{1,0:T(8,128)(2,1)} %reshape.129.refs_0_), channel_id=1, source_target_pairs={{0,2},{2,4},{4,6},{6,0},{1,3},{3,5},{5,7},{7,1},{8,10},{10,12},{12... | collective-permute-start | bytes 983048 | tf_op jit(solution)/shard_map/ppermute | solution.py:298
  29.2 17.5 %collective-permute-start.1 = (bf16[64,2560]{1,0:T(8,128)(2,1)}, bf16[64,2560]{1,0:T(8,128)(2,1)}, u32[]{:S(2)}, u32[]{:S(2)}) collective-permute-start(bf16[64,2560]{1,0:T(8,128)(2,1)} %reshape.129.refs_0_), channel_id=1, source_target_pairs={{0,4},{2,6},{4,0},{6,2},{1,5},{3,7},{5,1},{7,3},{8,12},{10,14},{12... | collective-permute-start | bytes 983048 | tf_op jit(solution)/shard_map/ppermute | solution.py:298
  32.8 14.0 %collective-permute-start.2 = (bf16[64,2560]{1,0:T(8,128)(2,1)}, bf16[64,2560]{1,0:T(8,128)(2,1)}, u32[]{:S(2)}, u32[]{:S(2)}) collective-permute-start(bf16[64,2560]{1,0:T(8,128)(2,1)} %reshape.129.refs_0_), channel_id=1, source_target_pairs={{0,6},{2,0},{4,2},{6,4},{1,7},{3,1},{5,3},{7,5},{8,14},{10,8},{12,... | collective-permute-start | bytes 983048 | tf_op jit(solution)/shard_map/ppermute | solution.py:298
  46.8 1.0 copy-start.9
  50.6 7.2 %collective-permute-start.3 = (bf16[256,2560]{1,0:T(8,128)(2,1)}, bf16[256,2560]{1,0:T(8,128)(2,1)}, u32[]{:S(2)}, u32[]{:S(2)}) collective-permute-start(bf16[256,2560]{1,0:T(8,128)(2,1)} %shard_map.76.hidden_ref.refs_0_), channel_id=1, source_target_pairs={{0,1},{1,0},{2,3},{3,2},{4,5},{5,4},{6,7},{7,6},{8,9},{9,8},{10,11... | collective-permute-start | bytes 3932168 | tf_op jit(solution)/shard_map/ppermute | solution.py:326
  50.7 2.1 %copy-start.1 = (bf16[2560,768]{1,0:T(8,128)(2,1)S(1)}, bf16[2560,768]{1,0:T(8,128)(2,1)}, u32[]{:S(2)}) copy-start(bf16[2560,768]{1,0:T(8,128)(2,1)} %head_ref.3) | copy-start | bytes 11796484
  52.8 5.0 %copy-start.2 = (bf16[2560,768]{1,0:T(8,128)(2,1)S(1)}, bf16[2560,768]{1,0:T(8,128)(2,1)}, u32[]{:S(2)}) copy-start(bf16[2560,768]{1,0:T(8,128)(2,1)} %head_ref.3) | copy-start | bytes 11796484
  56.9 0.9 copy-start.4
  61.6 0.9 copy-start.7
  62.5 3.7 %collective-permute-start.7 = (f32[4,512]{1,0:T(4,128)S(1)}, f32[4,512]{1,0:T(4,128)S(1)}, u32[]{:S(2)}, u32[]{:S(2)}) collective-permute-start(f32[4,512]{1,0:T(4,128)S(1)} %bitcast.91), channel_id=1, source_target_pairs={{0,6},{2,0},{4,2},{6,4},{1,7},{3,1},{5,3},{7,5},{8,14},{10,8},{12,... | collective-permute-start | bytes 24584 | tf_op jit(solution)/shard_map/ppermute | solution.py:336
  64.6 5.2 %collective-permute-start.6 = (f32[4,512]{1,0:T(4,128)S(1)}, f32[4,512]{1,0:T(4,128)S(1)}, u32[]{:S(2)}, u32[]{:S(2)}) collective-permute-start(f32[4,512]{1,0:T(4,128)S(1)} %bitcast.92), channel_id=1, source_target_pairs={{0,4},{2,6},{4,0},{6,2},{1,5},{3,7},{5,1},{7,3},{8,12},{10,14},{12... | collective-permute-start | bytes 24584 | tf_op jit(solution)/shard_map/ppermute | solution.py:336
  65.8 4.9 %collective-permute-start.5 = (f32[4,512]{1,0:T(4,128)S(1)}, f32[4,512]{1,0:T(4,128)S(1)}, u32[]{:S(2)}, u32[]{:S(2)}) collective-permute-start(f32[4,512]{1,0:T(4,128)S(1)} %bitcast.93), channel_id=1, source_target_pairs={{0,2},{2,4},{4,6},{6,0},{1,3},{3,5},{5,7},{7,1},{8,10},{10,12},{12... | collective-permute-start | bytes 24584 | tf_op jit(solution)/shard_map/ppermute | solution.py:336
  71.9 6.5 %collective-permute-start.8 = (f32[4,128]{1,0:T(4,128)S(1)}, f32[4,128]{1,0:T(4,128)S(1)}, u32[]{:S(2)}, u32[]{:S(2)}) collective-permute-start(f32[4,128]{1,0:T(4,128)S(1)} %bitcast.96), channel_id=1, source_target_pairs={{0,1},{1,0},{2,3},{3,2},{4,5},{5,4},{6,7},{7,6},{8,9},{9,8},{10,11... | collective-permute-start | bytes 6152 | tf_op jit(solution)/shard_map/ppermute | solution.py:340
  72.2 1.1 copy-start.5
  73.3 1.1 copy-start.8
  74.5 28.9 %copy-start.6 = (f32[256,768]{1,0:T(8,128)S(1)}, f32[256,768]{1,0:T(8,128)}, u32[]{:S(2)}) copy-start(f32[256,768]{1,0:T(8,128)} %copy-done.4) | copy-start | bytes 2359300
  77.8 27.9 %copy-start.3 = (bf16[2560,768]{1,0:T(8,128)(2,1)S(1)}, bf16[2560,768]{1,0:T(8,128)(2,1)}, u32[]{:S(2)}) copy-start(bf16[2560,768]{1,0:T(8,128)(2,1)} %head_ref.3) | copy-start | bytes 11796484
  77.8 1.4 collective-permute-start.4
  107.0 8.5 %collective-permute-start.9 = (f32[256,2560]{1,0:T(8,128)S(1)}, f32[256,2560]{1,0:T(8,128)S(1)}, u32[]{:S(2)}, u32[]{:S(2)}) collective-permute-start(f32[256,2560]{1,0:T(8,128)S(1)} %fusion.32), channel_id=1, source_target_pairs={{0,1},{1,0},{2,3},{3,2},{4,5},{5,4},{6,7},{7,6},{8,9},{9,8},{10,11... | collective-permute-start | bytes 7864328 | tf_op jit(solution)/shard_map/ppermute | solution.py:351

commit v5 on v4

--- a/solution.py
+++ b/solution.py
@@ -351,15 +351,14 @@
     taken = lax.ppermute(give, "c", pair)
     keep = lax.dot_general(own_grad, student_head, contract, preferred_element_type=jnp.float32)
     grad = jnp.concatenate([own_grad, other_grad], axis=0)
-    late = (jnp.abs(own_grad[0, 0].astype(jnp.float32)) > 3e38).astype(jnp.int32)
+    objective = objective[:2].T
+
+    share = (keep + taken).astype(jnp.bfloat16).reshape(chips, 4, width)
+    late = (jnp.abs(share[0, 0, 0].astype(jnp.float32)) > 3e38).astype(jnp.int32)
     hidden = place_blocks(jnp.arange(2, dtype=jnp.int32) + late, own, other)
     grad_head = lax.dot_general(
         hidden, grad, (((0,), (0,)), ((), ())), preferred_element_type=jnp.float32
     ).astype(jnp.bfloat16)
-    objective = objective[:2].T
-
-    share = (keep + taken).astype(jnp.bfloat16).reshape(chips, 4, width)
-    share, grad_head, objective = lax.optimization_barrier((share, grad_head, objective))
     share = lax.all_to_all(share, WALK, 0, 0, tiled=True)
     grad_hidden = jnp.sum(share.astype(jnp.float32), axis=0).astype(jnp.bfloat16)
     grad_hidden = jnp.swapaxes(grad_hidden.reshape(2, 2, width), 0, 1)

time: 146 us -> 144 us (0.986)
  blocking collectives: 50.6 us -> 23.4 us
  waiting for transfers between devices: 18.6 us -> 36.3 us
  starting transfers between devices: 24.9 us -> 30 us
  local copies, waits for them, and re-layouts: 15.1 us -> 17.3 us
    all_to_all x1 -> x0, blocking collectives: 27.1 us -> none  [local(): share = lax.all_to_all(share, WALK, 0, 0, tiled=True)]
    all_to_all x0 -> x1, waiting for transfers between devices: none -> 12.9 us  [local(): share = lax.all_to_all(share, WALK, 0, 0, tiled=True)]
    all_to_all x0 -> x1, starting transfers between devices: none -> 4.95 us  [local(): share = lax.all_to_all(share, WALK, 0, 0, tiled=True)]
    ppermute x1, waiting for transfers between devices: 0.01 us -> 4.9 us  [local(): taken = lax.ppermute(give, 'c', pair)]
    unnamed x23 -> x25, local copies, waits for them, and re-layouts: 7.78 us -> 8.49 us
  transfers between devices with their start and end apart: 12 -> 13, of which waited for: 6 -> 8; matrix products, arithmetic and copies ran while one was open for 11% -> 12% of each run, Pallas kernels for 11% -> 12%
where the time goes in v5:
time: 144 us; the launch traced here: 143 us
  waiting for transfers between devices  36.3 us (25%)
  starting transfers between devices  30 us (21%)
  blocking collectives  23.4 us (16%)
  Pallas kernels  19.5 us (14%)
  local copies, waits for them, and re-layouts  17.3 us (12%)
  matrix products  12.3 us (9%)
  between operations  2.19 us (2%)
  other arithmetic  2.15 us (1%)
    all_to_all x1, blocking collectives, local(): shares = lax.all_to_all(copies, EXCHANGE, 0, 0, tiled=True)  23.4 us
    pallas_call x7, Pallas kernels, call(): pl.pallas_call(kernel, out_shape=tuple(results), grid_spec=pltpu.Prefetch...  19.5 us
    all_to_all x1, waiting for transfers between devices, local(): share = lax.all_to_all(share, WALK, 0, 0, tiled=True)  12.9 us
    ppermute x3, waiting for transfers between devices, ring_gather(): lax.ppermute(block, axis, [(i, (i + step) % size) for i in range(size)])  12.9 us
    unnamed x25, local copies, waits for them, and re-layouts  8.49 us
    all_to_all x1, starting transfers between devices, everywhere(): return lax.all_to_all(copies, axes, 0, 0, tiled=True)  7.12 us
    all_to_all x1, starting transfers between devices, local(): words = lax.all_to_all(words, STRIPES, 0, 0, tiled=True)  6.74 us
    ppermute x3, starting transfers between devices, ring_gather(): lax.ppermute(block, axis, [(i, (i + step) % size) for i in range(size)])  6.49 us
  transfers between devices with their start and end apart: 13, of which 8 were waited for; matrix products, arithmetic and copies ran while one was open for 12% of the time, Pallas kernels for 12%

profile of v5, /device:TPU:0, one launch (start us, length us, event | category | flops | bytes accessed | tf_op | source)
XLA Modules:
  0.0 143.1 jit_solution(16944223871240147258)
XLA Ops:
  2.3 7.1 %all-to-all-start.1 = ((bf16[16,4,2560]{2,1,0:T(4,128)(2,1)}), bf16[16,4,2560]{2,1,0:T(4,128)(2,1)S(1)}, u32[]{:S(2)}, u32[]{:S(2)}) async-start(bf16[16,4,2560]{2,1,0:T(4,128)(2,1)} %broadcast_in_dim.2), calls=%async_computation.1 | async-start | bytes 655360 | tf_op jit(solution)/shard_map/all_to_all | solution.py:304
  9.4 5.7 %abs_reduce_fusion = (f32[8,256]{1,0:T(8,128)S(1)}, f32[8,768,256]{1,2,0:T(8,128)S(1)}) fusion(bf16[512,8,768]{2,1,0:T(8,128)(2,1)} %param.8, bf16[256,512]{1,0:T(8,128)(2,1)S(1)} %copy-done), kind=kOutput, calls=%fused_computation.3 | convolution fusion | flops 1613756416 | bytes 12853248 | tf_op jit(solution)/shard_map/rd,dsv->srv/dot_general | solution.py:317
  16.5 1.9 %copy.30 = s32[2,2,2,264,384]{4,3,0,1,2:T(8,128)} copy(s32[2,2,2,264,384]{4,3,2,1,0:T(8,128)S(1)} %bitcast.89) | data formatting | bytes 6488064 | tf_op jit(solution)/shard_map/reshape | solution.py:319
  19.5 6.7 %all-to-all-start = ((s32[8,264,384]{2,1,0:T(8,128)}), s32[8,264,384]{2,1,0:T(8,128)S(1)}, u32[]{:S(2)}, u32[]{:S(2)}) async-start(s32[8,264,384]{2,1,0:T(8,128)} %bitcast.88), calls=%async_computation | async-start | bytes 6488064 | tf_op jit(solution)/shard_map/all_to_all | solution.py:320
  26.2 1.8 %reshape.129.refs_0_ = bf16[64,2560]{1,0:T(8,128)(2,1)} reshape(bf16[16,4,2560]{2,1,0:T(4,128)(2,1)} %copy-done.10) | data formatting | bytes 655360 | tf_op jit(solution)/shard_map/reshape | solution.py:323
  28.0 1.9 %collective-permute-start = (bf16[64,2560]{1,0:T(8,128)(2,1)}, bf16[64,2560]{1,0:T(8,128)(2,1)}, u32[]{:S(2)}, u32[]{:S(2)}) collective-permute-start(bf16[64,2560]{1,0:T(8,128)(2,1)} %reshape.129.refs_0_), channel_id=1, source_target_pairs={{0,2},{2,4},{4,6},{6,0},{1,3},{3,5},{5,7},{7,1},{8,10},{10,12},{12... | collective-permute-start | bytes 983048 | tf_op jit(solution)/shard_map/ppermute | solution.py:298
  29.9 3.6 %collective-permute-start.1 = (bf16[64,2560]{1,0:T(8,128)(2,1)}, bf16[64,2560]{1,0:T(8,128)(2,1)}, u32[]{:S(2)}, u32[]{:S(2)}) collective-permute-start(bf16[64,2560]{1,0:T(8,128)(2,1)} %reshape.129.refs_0_), channel_id=1, source_target_pairs={{0,4},{2,6},{4,0},{6,2},{1,5},{3,7},{5,1},{7,3},{8,12},{10,14},{12... | collective-permute-start | bytes 983048 | tf_op jit(solution)/shard_map/ppermute | solution.py:298
  33.5 1.0 collective-permute-start.2
  34.5 5.6 %collective-permute-done.refs_1_ = bf16[64,2560]{1,0:T(8,128)(2,1)} collective-permute-done((bf16[64,2560]{1,0:T(8,128)(2,1)}, bf16[64,2560]{1,0:T(8,128)(2,1)}, u32[]{:S(2)}, u32[]{:S(2)}) %collective-permute-start) | collective-permute-done | bytes 327712 | tf_op jit(solution)/shard_map/ppermute | solution.py:298
  40.1 7.3 %collective-permute-done.1.refs_2_ = bf16[64,2560]{1,0:T(8,128)(2,1)} collective-permute-done((bf16[64,2560]{1,0:T(8,128)(2,1)}, bf16[64,2560]{1,0:T(8,128)(2,1)}, u32[]{:S(2)}, u32[]{:S(2)}) %collective-permute-start.1) | collective-permute-done | bytes 327712 | tf_op jit(solution)/shard_map/ppermute | solution.py:298
  47.4 1.0 copy-done.9
  48.4 2.9 %shard_map.76.hidden_ref.refs_0_ = bf16[256,2560]{1,0:T(8,128)(2,1)} custom-call(s32[4]{0:T(128)S(1)} %and_select_fusion.places_ref, bf16[64,2560]{1,0:T(8,128)(2,1)S(1)} %copy-done.9, bf16[64,2560]{1,0:T(8,128)(2,1)} %collective-permute-done.refs_1_, bf16[64,2560]{1,0:T(8,128)(2,1)} %collective-permute-done.1.refs_2_, ...), custom_call_target="tpu_custom_call" | custom-call | bytes 2621440 | tf_op jit(solution)/shard_map/pallas_call | solution.py:145
  51.4 2.1 %copy-done.1 = bf16[2560,768]{1,0:T(8,128)(2,1)S(1)} copy-done((bf16[2560,768]{1,0:T(8,128)(2,1)S(1)}, bf16[2560,768]{1,0:T(8,128)(2,1)}, u32[]{:S(2)}) %copy-start.1) | copy-done | bytes 3932184
  53.5 4.1 %shard_map.77 = (f32[256,768]{1,0:T(8,128)S(1)}, f32[8,256]{1,0:T(8,128)S(1)}) custom-call(s32[2]{0:T(128)S(1)} %pad_add_fusion.1.core_ref, bf16[256,2560]{1,0:T(8,128)(2,1)} %shard_map.76.hidden_ref.refs_0_, bf16[2560,768]{1,0:T(8,128)(2,1)S(1)} %copy-done.1, f32[2,256]{1,0:T(2,128)S(1)} %convert_bitcast_fusion.1.ids_ref), custom_call_target="tpu_custom_call" | custom-call | flops 1006632960 | bytes 4718592 | tf_op jit(solution)/shard_map/pallas_call | solution.py:145
  58.5 3.8 %shard_map.78 = (f32[256,768]{1,0:T(8,128)S(1)}, f32[8,256]{1,0:T(8,128)S(1)}) custom-call(s32[2]{0:T(128)S(1)} %pad_add_fusion.1.core_ref, bf16[256,2560]{1,0:T(8,128)(2,1)} %collective-permute-done.3.hidden_ref.refs_1_, bf16[2560,768]{1,0:T(8,128)(2,1)S(1)} %copy-done.2, f32[2,256]{1,0:T(2,128)S(1)} %convert_bitcast_fusion.1.ids_ref), custom_call_target="tpu_custom_call" | custom-call | flops 1006632960 | bytes 4718592 | tf_op jit(solution)/shard_map/pallas_call | solution.py:145
  63.2 2.1 %collective-permute-start.7 = (f32[4,512]{1,0:T(4,128)S(1)}, f32[4,512]{1,0:T(4,128)S(1)}, u32[]{:S(2)}, u32[]{:S(2)}) collective-permute-start(f32[4,512]{1,0:T(4,128)S(1)} %bitcast.91), channel_id=1, source_target_pairs={{0,6},{2,0},{4,2},{6,4},{1,7},{3,1},{5,3},{7,5},{8,14},{10,8},{12,... | collective-permute-start | bytes 24584 | tf_op jit(solution)/shard_map/ppermute | solution.py:336
  65.3 1.1 collective-permute-start.6
  66.9 3.6 %collective-permute-done.6 = f32[4,512]{1,0:T(4,128)S(1)} collective-permute-done((f32[4,512]{1,0:T(4,128)S(1)}, f32[4,512]{1,0:T(4,128)S(1)}, u32[]{:S(2)}, u32[]{:S(2)}) %collective-permute-start.6) | collective-permute-done | bytes 8224 | tf_op jit(solution)/shard_map/ppermute | solution.py:336
  72.9 1.1 copy-done.5
  74.0 1.1 copy-done.8
  75.1 3.3 %shard_map.79 = (f32[256,768]{1,0:T(8,128)S(1)}, f32[256,768]{1,0:T(8,128)S(1)}, f32[8,128]{1,0:T(8,128)S(1)}) custom-call(s32[2]{0:T(128)S(1)} %pad_add_fusion.1.core_ref, s32[8,264,384]{2,1,0:T(8,128)S(1)} %all-to-all-done.words_ref, f32[256,768]{1,0:T(8,128)S(1)} %copy-done.5, f32[256,768]{1,0:T(8,128)S(1)} %copy-done.8), custom_call_target="tpu_custom_call" | custom-call | flops 603979776 | bytes 7864320 | tf_op jit(solution)/shard_map/pallas_call | solution.py:145
  80.5 23.4 %all_to_all.20.shares_ref = f32[64,16,128]{2,1,0:T(8,128)S(1)} all-to-all(f32[64,16,128]{2,1,0:T(8,128)S(1)} %shard_map.80), channel_id=1, replica_groups=mesh['xh'=2,'xl'=2,'yh'=2,'yl'=2,'z'=4,'c'=2] {'z','yh','xh','yl','xl'}, dimensions={0} | all-to-all | bytes 1048576 | tf_op jit(solution)/shard_map/all_to_all | solution.py:344
  103.9 2.4 %shard_map.81 = (bf16[256,768]{1,0:T(8,128)(2,1)S(1)}, bf16[256,768]{1,0:T(8,128)(2,1)S(1)}, f32[8,256]{1,0:T(8,128)S(1)}) custom-call(s32[2]{0:T(128)S(1)} %pad_add_fusion.1.core_ref, f32[64,16,128]{2,1,0:T(8,128)S(1)} %all_to_all.20.shares_ref, f32[2,256]{1,0:T(2,128)S(1)} %convert_bitcast_fusion.1.ids_ref, f32[256,768]{1,0:T(8,128)S(1)} %copy-done.6, ...), custom_call_target="tpu_custom_call" | custom-call | flops 7864320 | bytes 4718592 | tf_op jit(solution)/shard_map/pallas_call | solution.py:145
  106.3 1.2 fusion.32
  107.6 4.9 %collective-permute-done.9 = f32[256,2560]{1,0:T(8,128)S(1)} collective-permute-done((f32[256,2560]{1,0:T(8,128)S(1)}, f32[256,2560]{1,0:T(8,128)S(1)}, u32[]{:S(2)}, u32[]{:S(2)}) %collective-permute-start.9) | collective-permute-done | bytes 2621472 | tf_op jit(solution)/shard_map/ppermute | solution.py:351
  112.5 1.2 fusion.2
  113.8 1.2 reshape.131
  115.0 5.0 %all-to-all-start.3 = ((bf16[64,4,2560]{2,1,0:T(4,128)(2,1)}), bf16[64,4,2560]{2,1,0:T(4,128)(2,1)S(1)}, u32[]{:S(2)}, u32[]{:S(2)}) async-start(bf16[64,4,2560]{2,1,0:T(4,128)(2,1)} %reshape.131), calls=%async_computation.3 | async-start | bytes 2621440 | tf_op jit(solution)/shard_map/all_to_all | solution.py:362
  120.5 1.2 slice.98
  122.4 2.4 %shard_map.82 = bf16[512,2560]{1,0:T(8,128)(2,1)S(1)} custom-call(s32[2]{0:T(128)S(1)} %iota_add_fusion.places_ref, bf16[256,2560]{1,0:T(8,128)(2,1)} %shard_map.76.hidden_ref.refs_0_, bf16[256,2560]{1,0:T(8,128)(2,1)} %collective-permute-done.3.hidden_ref.refs_1_), custom_call_target="tpu_custom_call" | custom-call | bytes 5242880 | tf_op jit(solution)/shard_map/pallas_call | solution.py:145
  124.8 4.2 %convolution_convert_fusion = bf16[2560,768]{1,0:T(8,128)(2,1)} fusion(bf16[512,2560]{1,0:T(8,128)(2,1)S(1)} %shard_map.82, bf16[256,768]{1,0:T(8,128)(2,1)S(1)} %get-tuple-element.34, bf16[256,768]{1,0:T(8,128)(2,1)S(1)} %get-tuple-element.33), kind=kOutput, calls=%fused_computation.4 | convolution fusion | flops 2016804864 | bytes 7340032 | tf_op jit(solution)/shard_map/dot_general | solution.py:359
  129.0 12.9 %all-to-all-done.3 = bf16[64,4,2560]{2,1,0:T(4,128)(2,1)S(1)} async-done(((bf16[64,4,2560]{2,1,0:T(4,128)(2,1)}), bf16[64,4,2560]{2,1,0:T(4,128)(2,1)S(1)}, u32[]{:S(2)}, u32[]{:S(2)}) %all-to-all-start.3) | async-done | bytes 1310752 | tf_op jit(solution)/shard_map/all_to_all | solution.py:362
  (60 shorter events, 12.0 us)
Async XLA Ops:
  0.6 8.8 %copy-start = (bf16[256,512]{1,0:T(8,128)(2,1)S(1)}, bf16[256,512]{1,0:T(8,128)(2,1)}, u32[]{:S(2)}) copy-start(bf16[256,512]{1,0:T(8,128)(2,1)} %param.7) | copy-start | bytes 786436
  2.3 16.5 %all-to-all-start.1 = ((bf16[16,4,2560]{2,1,0:T(4,128)(2,1)}), bf16[16,4,2560]{2,1,0:T(4,128)(2,1)S(1)}, u32[]{:S(2)}, u32[]{:S(2)}) async-start(bf16[16,4,2560]{2,1,0:T(4,128)(2,1)} %broadcast_in_dim.2), calls=%async_computation.1 | async-start | bytes 655360 | tf_op jit(solution)/shard_map/all_to_all | solution.py:304
  18.8 0.7 copy-start.10
  19.5 51.9 %all-to-all-start = ((s32[8,264,384]{2,1,0:T(8,128)}), s32[8,264,384]{2,1,0:T(8,128)S(1)}, u32[]{:S(2)}, u32[]{:S(2)}) async-start(s32[8,264,384]{2,1,0:T(8,128)} %bitcast.88), calls=%async_computation | async-start | bytes 6488064 | tf_op jit(solution)/shard_map/all_to_all | solution.py:320
  26.2 25.1 %copy-start.11 = (s32[256,2]{0,1:T(2,128)S(1)}, s32[256,2]{0,1:T(2,128)}, u32[]{:S(2)}) copy-start(s32[256,2]{0,1:T(2,128)} %param.11) | copy-start | bytes 6148
  28.0 12.1 %collective-permute-start = (bf16[64,2560]{1,0:T(8,128)(2,1)}, bf16[64,2560]{1,0:T(8,128)(2,1)}, u32[]{:S(2)}, u32[]{:S(2)}) collective-permute-start(bf16[64,2560]{1,0:T(8,128)(2,1)} %reshape.129.refs_0_), channel_id=1, source_target_pairs={{0,2},{2,4},{4,6},{6,0},{1,3},{3,5},{5,7},{7,1},{8,10},{10,12},{12... | collective-permute-start | bytes 983048 | tf_op jit(solution)/shard_map/ppermute | solution.py:298
  29.9 17.5 %collective-permute-start.1 = (bf16[64,2560]{1,0:T(8,128)(2,1)}, bf16[64,2560]{1,0:T(8,128)(2,1)}, u32[]{:S(2)}, u32[]{:S(2)}) collective-permute-start(bf16[64,2560]{1,0:T(8,128)(2,1)} %reshape.129.refs_0_), channel_id=1, source_target_pairs={{0,4},{2,6},{4,0},{6,2},{1,5},{3,7},{5,1},{7,3},{8,12},{10,14},{12... | collective-permute-start | bytes 983048 | tf_op jit(solution)/shard_map/ppermute | solution.py:298
  33.5 13.9 %collective-permute-start.2 = (bf16[64,2560]{1,0:T(8,128)(2,1)}, bf16[64,2560]{1,0:T(8,128)(2,1)}, u32[]{:S(2)}, u32[]{:S(2)}) collective-permute-start(bf16[64,2560]{1,0:T(8,128)(2,1)} %reshape.129.refs_0_), channel_id=1, source_target_pairs={{0,6},{2,0},{4,2},{6,4},{1,7},{3,1},{5,3},{7,5},{8,14},{10,8},{12,... | collective-permute-start | bytes 983048 | tf_op jit(solution)/shard_map/ppermute | solution.py:298
  47.4 1.0 copy-start.9
  51.3 7.2 %collective-permute-start.3 = (bf16[256,2560]{1,0:T(8,128)(2,1)}, bf16[256,2560]{1,0:T(8,128)(2,1)}, u32[]{:S(2)}, u32[]{:S(2)}) collective-permute-start(bf16[256,2560]{1,0:T(8,128)(2,1)} %shard_map.76.hidden_ref.refs_0_), channel_id=1, source_target_pairs={{0,1},{1,0},{2,3},{3,2},{4,5},{5,4},{6,7},{7,6},{8,9},{9,8},{10,11... | collective-permute-start | bytes 3932168 | tf_op jit(solution)/shard_map/ppermute | solution.py:326
  51.4 2.1 %copy-start.1 = (bf16[2560,768]{1,0:T(8,128)(2,1)S(1)}, bf16[2560,768]{1,0:T(8,128)(2,1)}, u32[]{:S(2)}) copy-start(bf16[2560,768]{1,0:T(8,128)(2,1)} %head_ref.3) | copy-start | bytes 11796484
  53.5 5.0 %copy-start.2 = (bf16[2560,768]{1,0:T(8,128)(2,1)S(1)}, bf16[2560,768]{1,0:T(8,128)(2,1)}, u32[]{:S(2)}) copy-start(bf16[2560,768]{1,0:T(8,128)(2,1)} %head_ref.3) | copy-start | bytes 11796484
  57.6 0.9 copy-start.4
  62.3 0.9 copy-start.7
  63.2 3.7 %collective-permute-start.7 = (f32[4,512]{1,0:T(4,128)S(1)}, f32[4,512]{1,0:T(4,128)S(1)}, u32[]{:S(2)}, u32[]{:S(2)}) collective-permute-start(f32[4,512]{1,0:T(4,128)S(1)} %bitcast.91), channel_id=1, source_target_pairs={{0,6},{2,0},{4,2},{6,4},{1,7},{3,1},{5,3},{7,5},{8,14},{10,8},{12,... | collective-permute-start | bytes 24584 | tf_op jit(solution)/shard_map/ppermute | solution.py:336
  65.3 5.2 %collective-permute-start.6 = (f32[4,512]{1,0:T(4,128)S(1)}, f32[4,512]{1,0:T(4,128)S(1)}, u32[]{:S(2)}, u32[]{:S(2)}) collective-permute-start(f32[4,512]{1,0:T(4,128)S(1)} %bitcast.92), channel_id=1, source_target_pairs={{0,4},{2,6},{4,0},{6,2},{1,5},{3,7},{5,1},{7,3},{8,12},{10,14},{12... | collective-permute-start | bytes 24584 | tf_op jit(solution)/shard_map/ppermute | solution.py:336
  66.4 4.9 %collective-permute-start.5 = (f32[4,512]{1,0:T(4,128)S(1)}, f32[4,512]{1,0:T(4,128)S(1)}, u32[]{:S(2)}, u32[]{:S(2)}) collective-permute-start(f32[4,512]{1,0:T(4,128)S(1)} %bitcast.93), channel_id=1, source_target_pairs={{0,2},{2,4},{4,6},{6,0},{1,3},{3,5},{5,7},{7,1},{8,10},{10,12},{12... | collective-permute-start | bytes 24584 | tf_op jit(solution)/shard_map/ppermute | solution.py:336
  72.6 6.5 %collective-permute-start.8 = (f32[4,128]{1,0:T(4,128)S(1)}, f32[4,128]{1,0:T(4,128)S(1)}, u32[]{:S(2)}, u32[]{:S(2)}) collective-permute-start(f32[4,128]{1,0:T(4,128)S(1)} %bitcast.96), channel_id=1, source_target_pairs={{0,1},{1,0},{2,3},{3,2},{4,5},{5,4},{6,7},{7,6},{8,9},{9,8},{10,11... | collective-permute-start | bytes 6152 | tf_op jit(solution)/shard_map/ppermute | solution.py:340
  72.9 1.1 copy-start.5
  74.0 1.1 copy-start.8
  75.1 28.8 %copy-start.6 = (f32[256,768]{1,0:T(8,128)S(1)}, f32[256,768]{1,0:T(8,128)}, u32[]{:S(2)}) copy-start(f32[256,768]{1,0:T(8,128)} %copy-done.4) | copy-start | bytes 2359300
  78.5 27.8 %copy-start.3 = (bf16[2560,768]{1,0:T(8,128)(2,1)S(1)}, bf16[2560,768]{1,0:T(8,128)(2,1)}, u32[]{:S(2)}) copy-start(bf16[2560,768]{1,0:T(8,128)(2,1)} %head_ref.3) | copy-start | bytes 11796484
  78.5 1.4 collective-permute-start.4
  107.5 5.0 %collective-permute-start.9 = (f32[256,2560]{1,0:T(8,128)S(1)}, f32[256,2560]{1,0:T(8,128)S(1)}, u32[]{:S(2)}, u32[]{:S(2)}) collective-permute-start(f32[256,2560]{1,0:T(8,128)S(1)} %fusion.32), channel_id=1, source_target_pairs={{0,1},{1,0},{2,3},{3,2},{4,5},{5,4},{6,7},{7,6},{8,9},{9,8},{10,11... | collective-permute-start | bytes 7864328 | tf_op jit(solution)/shard_map/ppermute | solution.py:351
  115.0 26.9 %all-to-all-start.3 = ((bf16[64,4,2560]{2,1,0:T(4,128)(2,1)}), bf16[64,4,2560]{2,1,0:T(4,128)(2,1)S(1)}, u32[]{:S(2)}, u32[]{:S(2)}) async-start(bf16[64,4,2560]{2,1,0:T(4,128)(2,1)} %reshape.131), calls=%async_computation.3 | async-start | bytes 2621440 | tf_op jit(solution)/shard_map/all_to_all | solution.py:362
